TPU v7x, 256 devices: a whole 4x4x8 slice. The times are simulated.
256 devices in a mesh: space: 32 (over z, x), batch: 8 (over y, core).
Axes of the slice: x: 4, y: 4, z: 8, core: 2. Of those that a mesh axis runs over, the one named last changes fastest.
Arguments:
- cotangent: float32 [16, 192, 128, 384], P('batch', 'space'), may hold values from -6 to 6
- grid_state: bfloat16 [16, 256, 128, 512], P('batch', 'space'), may hold values from -6 to 6
- legendre: bfloat16 [192, 192, 256], P('space'), may hold values from -0.375 to 0.375
- inverse: float32 [192, 4, 32, 32], P('space'), may hold values from -1 to 1
- gauss_weights: float32 [256], replicated, may hold values from 0.5 to 1.5
- w_in: bfloat16 [128, 256], replicated, may hold values from -0.5 to 0.5
- bias_in: float32 [256], replicated, may hold values from -3 to 3
- w_mid: bfloat16 [256, 256], replicated, may hold values from -0.375 to 0.375
- bias_mid: float32 [256], replicated, may hold values from -3 to 3
- w_out: bfloat16 [256, 128], replicated, may hold values from -0.5 to 0.5
Outputs:
- grad_state: float32 [16, 192, 128, 384], P('batch', 'space')
- grad_w_in: float32 [128, 256], replicated
- grad_bias_in: float32 [256], replicated
- grad_w_mid: float32 [256, 256], replicated
- grad_bias_mid: float32 [256], replicated
- grad_w_out: float32 [256, 128], replicated
All inputs are finite; a program needn't handle non-finite values.
Results may differ from a plain program's by a relative error of at most 0.0075.
Values may be sent and summed in bfloat16 or wider, within the bound.
A program may use at most 128 MiB of HBM per device.

v0:
```python
import math

import jax
import jax.numpy as jnp
from jax import lax
from jax.sharding import PartitionSpec as P


def fourier_table(waves, longitudes):
    wave_ids = jnp.arange(waves, dtype=jnp.int32)[:, None]
    columns = jnp.arange(longitudes, dtype=jnp.int32)[None, :]
    phase = (wave_ids * columns % longitudes).astype(jnp.float32) * (2.0 * math.pi / longitudes)
    scale = 1.0 / math.sqrt(waves)
    return jnp.stack([jnp.cos(phase) * scale, -jnp.sin(phase) * scale]).astype(jnp.bfloat16)


def gelu_value(v):
    inner = 0.7978845608 * (v + 0.044715 * v * v * v)
    return 0.5 * v * (1.0 + jnp.tanh(inner))


def gelu_slope(v):
    tanh_part = jnp.tanh(0.7978845608 * (v + 0.044715 * v * v * v))
    return 0.5 * (1.0 + tanh_part) + 0.5 * v * (1.0 - tanh_part * tanh_part) * 0.7978845608 * (
        1.0 + 0.134145 * v * v
    )


def shards(
    cotangent, grid_state, legendre, inverse, gauss_weights, w_in, bias_in, w_mid, bias_mid, w_out
):
    trajs, wave_dev, channels, coeffs = cotangent.shape
    fields = inverse.shape[1]
    levels = inverse.shape[2]
    degrees = coeffs // 2
    lat_rows = grid_state.shape[1]
    longitudes = grid_state.shape[3]
    waves = wave_dev * lax.axis_size("space")
    hidden_units = w_in.shape[1]
    table = fourier_table(waves, longitudes)
    cot_fields = cotangent.reshape(trajs, wave_dev, fields, levels, coeffs)
    spec_grad = jnp.einsum(
        "mfjk,bmfjl->bmfkl", inverse, cot_fields, precision=lax.Precision.HIGHEST
    )
    spec_grad = spec_grad.reshape(trajs, wave_dev, channels, coeffs)
    spec_half = spec_grad.astype(jnp.bfloat16).reshape(trajs, wave_dev, channels, 2, degrees)
    summed = jnp.einsum("bmkcl,mla->mabck", spec_half, legendre, preferred_element_type=jnp.float32)
    wave_grad = (summed * gauss_weights[None, :, None, None, None]).astype(jnp.bfloat16)
    wave_grad = wave_grad.reshape(wave_dev, wave_grad.shape[1], trajs * 2 * channels)
    arrived = lax.all_to_all(wave_grad, "space", split_axis=1, concat_axis=0, tiled=True)
    parts = arrived.reshape(waves, lat_rows, trajs, 2, channels)
    tend_grad = jnp.einsum(
        "mabck,cmo->bako", parts, table, preferred_element_type=jnp.float32
    ).astype(jnp.bfloat16)
    pre_in = jnp.einsum("kh,bako->baho", w_in, grid_state, preferred_element_type=jnp.float32)
    pre_in = pre_in + bias_in[None, None, :, None]
    hidden_in = gelu_value(pre_in).astype(jnp.bfloat16)
    pre_mid = jnp.einsum("hg,baho->bago", w_mid, hidden_in, preferred_element_type=jnp.float32)
    pre_mid = pre_mid + bias_mid[None, None, :, None]
    hidden_mid = gelu_value(pre_mid).astype(jnp.bfloat16)
    out_raw = jnp.einsum("bago,bako->gk", hidden_mid, tend_grad, preferred_element_type=jnp.float32)
    back_mid = jnp.einsum("gk,bako->bago", w_out, tend_grad, preferred_element_type=jnp.float32)
    err_mid = (back_mid * gelu_slope(pre_mid)).astype(jnp.bfloat16)
    mid_raw = jnp.einsum("baho,bago->hg", hidden_in, err_mid, preferred_element_type=jnp.float32)
    bmid_raw = jnp.sum(err_mid.astype(jnp.float32), axis=(0, 1, 3))
    back_in = jnp.einsum("hg,bago->baho", w_mid, err_mid, preferred_element_type=jnp.float32)
    err_in = (back_in * gelu_slope(pre_in)).astype(jnp.bfloat16)
    in_raw = jnp.einsum("bako,baho->kh", grid_state, err_in, preferred_element_type=jnp.float32)
    bin_raw = jnp.sum(err_in.astype(jnp.float32), axis=(0, 1, 3))
    in_raw, bin_raw, mid_raw, bmid_raw, out_raw = lax.psum(
        (in_raw, bin_raw, mid_raw, bmid_raw, out_raw), ("space", "batch")
    )
    state_grid = jnp.einsum(
        "kh,baho->bako", w_in, err_in, preferred_element_type=jnp.float32
    ).astype(jnp.bfloat16)
    wave_back = jnp.einsum(
        "bako,cmo->mabck", state_grid, table, preferred_element_type=jnp.float32
    ).astype(jnp.bfloat16)
    wave_back = wave_back.reshape(waves, lat_rows, trajs * 2 * channels)
    returned = lax.all_to_all(wave_back, "space", split_axis=0, concat_axis=1, tiled=True)
    spectral = jnp.einsum("mai,mla->mli", returned, legendre, preferred_element_type=jnp.float32)
    spectral = spectral.reshape(wave_dev, degrees, trajs, 2, channels)
    spectral = spectral.transpose(2, 0, 4, 3, 1).reshape(trajs, wave_dev, channels, 2 * degrees)
    grad_state = spec_grad + spectral
    total = jnp.sum(in_raw * in_raw) + jnp.sum(bin_raw * bin_raw) + jnp.sum(mid_raw * mid_raw)
    total = total + jnp.sum(bmid_raw * bmid_raw) + jnp.sum(out_raw * out_raw)
    limit = math.sqrt(2 * channels * hidden_units + hidden_units * hidden_units + 2 * hidden_units)
    factor = jnp.minimum(jnp.float32(1.0), limit / jnp.sqrt(total + 1e-06))
    return (
        grad_state,
        factor * in_raw,
        factor * bin_raw,
        factor * mid_raw,
        factor * bmid_raw,
        factor * out_raw,
    )


def solution(mesh):
    return jax.shard_map(
        shards,
        mesh=mesh,
        in_specs=(
            P("batch", "space", None, None),
            P("batch", "space", None, None),
            P("space", None, None),
            P("space", None, None, None),
            P(),
            P(),
            P(),
            P(),
            P(),
            P(),
        ),
        out_specs=(P("batch", "space", None, None), P(), P(), P(), P(), P()),
        check_vma=False,
    )
```

profile of v0, /device:TPU:1, one launch (start us, length us, event | category | flops | bytes accessed | tf_op | source)
XLA Modules:
  0.0 422.6 jit_solution(10532567406521121343)
XLA Ops:
  7.2 0.0 copy-start
  7.2 0.0 copy-start.5
  7.2 5.4 %fusion.77 = (bf16[2,6,4,32,384]{4,3,0,2,1:T(8,128)(2,1)S(1)}, f32[2,6,4,32,384]{4,3,0,2,1:T(8,128)}) fusion(f32[6,4,32,32]{3,2,1,0:T(8,128)} %param.13, f32[2,6,4,32,384]{4,3,2,1,0:T(8,128)} %bitcast.143), kind=kOutput, calls=%fused_computation.89 | convolution fusion | flops 227082240 | bytes 5996544 | tf_op jit(solution)/shard_map/mfjk,bmfjl->bmfkl/dot_general | solution.py:42
  12.6 0.2 copy.52
  12.8 1.8 convert_element_type.68
  14.5 0.0 copy-done.5
  14.5 3.3 multiply_convert_fusion.2
  17.8 4.5 %copy.54 = bf16[6,256,512]{2,0,1:T(8,128)(2,1)} copy(bf16[6,256,512]{1,2,0:T(8,128)(2,1)} %bitcast.145) | data formatting | bytes 3145728 | tf_op jit(solution)/shard_map/reshape | solution.py:49
  22.3 12.2 %all-to-all-start = ((bf16[6,256,512]{2,0,1:T(8,128)(2,1)}), bf16[6,256,512]{2,0,1:T(8,128)(2,1)}, u32[]{:S(2)}, u32[]{:S(2)}) async-start(bf16[6,256,512]{2,0,1:T(8,128)(2,1)} %copy.54), calls=%async_computation | async-start | bytes 4194304 | tf_op jit(solution)/shard_map/all_to_all | solution.py:50
  34.5 1.7 multiply_convert_fusion.3
  36.1 0.0 copy-done
  36.1 0.0 copy-done.4
  36.2 0.0 copy-done.7
  36.2 0.0 copy-start.2
  36.2 0.0 copy-start.6
  36.2 5.3 %multiply_convert_fusion.1 = (bf16[2,8,256,512]{2,3,1,0:T(8,128)(2,1)S(1)}, f32[2,8,512,256]{3,2,1,0:T(8,128)}) fusion(f32[256]{0:T(256)S(1)} %copy-done.7, bf16[2,8,128,512]{3,2,1,0:T(8,128)(2,1)S(1)} %copy-done, bf16[128,256]{1,0:T(8,128)(2,1)S(1)} %copy-done.4), kind=kOutput, calls=%fused_computation.23 | convolution fusion | flops 557842432 | bytes 14746624 | tf_op jit(solution)/shard_map/kh,bako->baho/dot_general | solution.py:55
  41.5 1.9 copy-done.10
  43.4 0.0 copy-done.2
  43.4 0.0 copy-done.6
  43.4 6.1 %multiply_convert_fusion = (bf16[2,8,256,512]{2,3,1,0:T(8,128)(2,1)}, f32[2,8,512,256]{3,2,1,0:T(8,128)}) fusion(f32[256]{0:T(256)S(1)} %copy-done.6, bf16[2,8,256,512]{2,3,1,0:T(8,128)(2,1)S(1)} %get-tuple-element.29, bf16[256,256]{1,0:T(8,128)(2,1)S(1)} %copy-done.2), kind=kOutput, calls=%fused_computation.20 | convolution fusion | flops 1094713344 | bytes 16909312 | tf_op jit(solution)/shard_map/hg,baho->bago/dot_general | solution.py:58
  49.5 33.3 %all-to-all-done = bf16[6,256,512]{2,0,1:T(8,128)(2,1)} async-done(((bf16[6,256,512]{2,0,1:T(8,128)(2,1)}), bf16[6,256,512]{2,0,1:T(8,128)(2,1)}, u32[]{:S(2)}, u32[]{:S(2)}) %all-to-all-start) | async-done | bytes 1572896 | tf_op jit(solution)/shard_map/all_to_all | solution.py:50
  82.8 2.4 copy.56
  85.2 0.0 copy-start.3
  85.2 0.0 slice-start
  85.2 1.3 fusion.36
  86.6 0.0 copy-start.9
  86.6 0.2 copy-done.14
  86.8 0.0 copy-done.3
  86.8 6.2 %convert_reduce_fusion = (f32[256]{0:T(256)S(1)}, bf16[2,8,256,512]{2,3,1,0:T(8,128)(2,1)S(1)}) fusion(f32[2,8,512,256]{3,2,1,0:T(8,128)S(1)} %copy-done.14, f32[256]{0:T(256)S(1)} %copy-done.6, bf16[256,128]{1,0:T(8,128)(2,1)S(1)} %copy-done.3, bf16[2,8,128,512]{2,3,0,1:T(8,128)(2,1)S(1)} %fusion.36), kind=kOutput, calls=%fused_computation.21 | convolution fusion | flops 583008000 | bytes 14747648 | tf_op jit(solution)/shard_map/gk,bako->bago/dot_general | solution.py:62
  93.0 0.0 copy-done.9
  93.0 0.0 copy-start.12
  93.1 7.6 %convert_reduce_fusion.1 = (f32[256]{0:T(256)S(1)}, bf16[2,8,256,512]{2,3,1,0:T(8,128)(2,1)}) fusion(f32[2,8,512,256]{3,2,1,0:T(8,128)S(1)} %bitcast.147, f32[256]{0:T(256)S(1)} %copy-done.7, bf16[2,8,256,512]{2,3,1,0:T(8,128)(2,1)S(1)} %get-tuple-element.38, bf16[256,256]{1,0:T(8,128)(2,1)S(1)} %copy-done.2), kind=kOutput, calls=%fused_computation.22 | convolution fusion | flops 1119878912 | bytes 16910336 | tf_op jit(solution)/shard_map/hg,bago->baho/dot_general | solution.py:66
  100.7 0.0 copy-done.12
  100.7 5.9 %fusion.41 = bf16[192,8,2,2,128]{4,0,1,2,3:T(8,128)(2,1)} fusion(bf16[2,8,256,512]{2,3,1,0:T(8,128)(2,1)} %get-tuple-element.36, bf16[1,192,512]{2,1,0:T(8,128)(2,1)S(1)} %get-tuple-element.39, bf16[1,192,512]{2,1,0:T(8,128)(2,1)S(1)} %get-tuple-element.40, bf16[128,256]{1,0:T(8,128)(2,1)S(1)} %copy-done.4), kind=kOutput, calls=%fused_computation.50 | convolution fusion | flops 1344798720 | bytes 6225920 | tf_op jit(solution)/shard_map/bako,cmo->mabck/dot_general | solution.py:76
  106.5 3.6 copy.61
  110.1 6.7 %all-to-all-start.1 = ((bf16[192,8,512]{2,1,0:T(8,128)(2,1)}), bf16[192,8,512]{2,1,0:T(8,128)(2,1)}, u32[]{:S(2)}, u32[]{:S(2)}) async-start(bf16[192,8,512]{2,1,0:T(8,128)(2,1)} %bitcast.142), calls=%async_computation.1 | async-start | bytes 3145728 | tf_op jit(solution)/shard_map/all_to_all | solution.py:80
  116.8 0.0 all-reduce.4.cloned.1.call-start
  116.9 5.0 %fusion.54 = f32[256,128]{1,0:T(8,128)} fusion(bf16[2,8,128,512]{2,3,0,1:T(8,128)(2,1)} %copy-done.9, bf16[2,8,256,512]{2,3,1,0:T(8,128)(2,1)} %get-tuple-element.33), kind=kOutput, calls=%fused_computation.53 | convolution fusion | flops 536870912 | bytes 6422528 | tf_op jit(solution)/shard_map/bago,bako->gk/dot_general | solution.py:61
  121.9 1.9 fusion.49
  123.8 0.2 copy-done.11
  124.1 1.3 copy-done.13
  125.4 2.0 fusion.44
  127.4 0.0 all-reduce.4.cloned.1.call-update
  127.4 3.3 copy.51
  130.7 81.3 %all-reduce = (f32[256]{0:T(256)S(1)}, f32[256]{0:T(256)S(1)}) all-reduce(f32[256]{0:T(256)S(1)} %get-tuple-element.35, f32[256]{0:T(256)S(1)} %get-tuple-element.37), channel_id=1, replica_groups=mesh['space'=32,'batch'=8] {'space','batch'}, use_global_device_ids=true, to_apply=%region_3.4 | all-reduce | flops 512 | bytes 4096 | tf_op jit(solution)/shard_map/psum | solution.py:70
  212.0 0.6 multiply_reduce_fusion.3
  212.6 0.6 multiply_reduce_fusion.4
  213.2 170.8 %all-reduce.4.cloned.1.call-done = (f32[128,256]{0,1:T(8,128)}, f32[256,256]{1,0:T(8,128)}, f32[256,128]{1,0:T(8,128)}) async-done(((f32[128,256]{0,1:T(8,128)}, f32[256,256]{1,0:T(8,128)}, f32[256,128]{1,0:T(8,128)}), (f32[128,256]{0,1:T(8,128)}, f32[256,256]{1,0:T(8,128)}, f32[256,128]{1,0:T(8,128)})) %all-reduce.4.cloned.1.call-update) | async-done | bytes 524304 | tf_op jit(solution)/shard_map/psum | solution.py:70
  384.0 1.5 multiply_reduce_fusion.2
  386.8 1.6 multiply_reduce_fusion
  389.8 1.5 multiply_reduce_fusion.1
  392.0 0.9 broadcast_multiply_fusion.2
  392.9 0.8 copy.71
  393.7 0.6 broadcast_multiply_fusion.3
  394.2 0.6 broadcast_multiply_fusion.4
  394.8 1.6 broadcast_multiply_fusion.1
  396.4 1.7 broadcast_multiply_fusion
  398.0 0.0 all-to-all-done.1
  398.0 0.0 copy-done.1
  398.0 3.3 convolution_bitcast_fusion
  401.3 3.9 reshape.122
  405.3 3.4 copy.63
  408.6 3.1 copy.64
  411.7 4.0 bitcast_add_fusion
  (13 shorter events, 0.0 us)
Async XLA Ops:
  7.2 29.0 %copy-start = (bf16[2,8,128,512]{3,2,1,0:T(8,128)(2,1)S(1)}, bf16[2,8,128,512]{3,2,1,0:T(8,128)(2,1)}, u32[]{:S(2)}) copy-start(bf16[2,8,128,512]{3,2,1,0:T(8,128)(2,1)} %param.11) | copy-start | bytes 6291460
  7.2 7.4 %copy-start.5 = (f32[256]{0:T(256)S(1)}, f32[256]{0:T(256)}, u32[]{:S(2)}) copy-start(f32[256]{0:T(256)} %param.14) | copy-start | bytes 3076
  17.8 18.4 %copy-start.4 = (bf16[128,256]{1,0:T(8,128)(2,1)S(1)}, bf16[128,256]{1,0:T(8,128)(2,1)}, u32[]{:S(2)}) copy-start(bf16[128,256]{1,0:T(8,128)(2,1)} %param.15) | copy-start | bytes 196612
  17.8 18.4 %copy-start.7 = (f32[256]{0:T(256)S(1)}, f32[256]{0:T(256)}, u32[]{:S(2)}) copy-start(f32[256]{0:T(256)} %param.16) | copy-start | bytes 3076
  22.3 60.5 %all-to-all-start = ((bf16[6,256,512]{2,0,1:T(8,128)(2,1)}), bf16[6,256,512]{2,0,1:T(8,128)(2,1)}, u32[]{:S(2)}, u32[]{:S(2)}) async-start(bf16[6,256,512]{2,0,1:T(8,128)(2,1)} %copy.54), calls=%async_computation | async-start | bytes 4194304 | tf_op jit(solution)/shard_map/all_to_all | solution.py:50
  36.2 7.2 %copy-start.2 = (bf16[256,256]{1,0:T(8,128)(2,1)S(1)}, bf16[256,256]{1,0:T(8,128)(2,1)}, u32[]{:S(2)}) copy-start(bf16[256,256]{1,0:T(8,128)(2,1)} %param.17) | copy-start | bytes 393220
  36.2 7.2 %copy-start.6 = (f32[256]{0:T(256)S(1)}, f32[256]{0:T(256)}, u32[]{:S(2)}) copy-start(f32[256]{0:T(256)} %param.18) | copy-start | bytes 3076
  41.5 1.9 copy-start.10
  82.8 4.0 copy-start.14
  85.2 1.6 copy-start.3
  85.2 7.8 %slice-start = ((s8[8388608]{0:T(1024)(128)(4,1)}), s8[4194304]{0:T(1024)(128)(4,1)S(1)}, s32[]{:S(2)}) async-start(s8[8388608]{0:T(1024)(128)(4,1)} %bitcast.146), calls=%async_computation.3 | async-start | bytes 8388608
  86.6 6.5 %copy-start.9 = (bf16[2,8,128,512]{2,3,0,1:T(8,128)(2,1)}, bf16[2,8,128,512]{2,3,0,1:T(8,128)(2,1)S(1)}, u32[]{:S(2)}) copy-start(bf16[2,8,128,512]{2,3,0,1:T(8,128)(2,1)S(1)} %fusion.36) | copy-start | bytes 6291460
  86.8 6.2 %slice-start.1 = ((s8[8388608]{0:T(1024)(128)(4,1)}), s8[4194304]{0:T(1024)(128)(4,1)S(1)}, s32[]{:S(2)}) async-start(s8[8388608]{0:T(1024)(128)(4,1)} %bitcast.146), calls=%async_computation.4 | async-start | bytes 8388608
  93.0 7.6 %copy-start.12 = (bf16[2,8,256,512]{2,3,1,0:T(8,128)(2,1)}, bf16[2,8,256,512]{2,3,1,0:T(8,128)(2,1)S(1)}, u32[]{:S(2)}) copy-start(bf16[2,8,256,512]{2,3,1,0:T(8,128)(2,1)S(1)} %get-tuple-element.38) | copy-start | bytes 12582916
  110.1 287.9 %all-to-all-start.1 = ((bf16[192,8,512]{2,1,0:T(8,128)(2,1)}), bf16[192,8,512]{2,1,0:T(8,128)(2,1)}, u32[]{:S(2)}, u32[]{:S(2)}) async-start(bf16[192,8,512]{2,1,0:T(8,128)(2,1)} %bitcast.142), calls=%async_computation.1 | async-start | bytes 3145728 | tf_op jit(solution)/shard_map/all_to_all | solution.py:80
  116.8 267.1 %all-reduce.4.cloned.1.call-start = ((), (), s32[]{:S(2)}) async-start(), calls=%async_computation.2 | async-start | bytes 1048576 | tf_op jit(solution)/shard_map/psum | solution.py:70
  116.9 5.0 %copy-start.8 = (bf16[2,8,256,512]{2,3,1,0:T(8,128)(2,1)S(1)}, bf16[2,8,256,512]{2,3,1,0:T(8,128)(2,1)}, u32[]{:S(2)}) copy-start(bf16[2,8,256,512]{2,3,1,0:T(8,128)(2,1)} %get-tuple-element.36) | copy-start | bytes 12582916
  121.9 2.2 copy-start.11
  121.9 3.5 copy-start.13
  127.4 270.7 %copy-start.1 = (bf16[6,192,256]{2,1,0:T(8,128)(2,1)S(1)}, bf16[6,192,256]{2,1,0:T(8,128)(2,1)}, u32[]{:S(2)}) copy-start(bf16[6,192,256]{2,1,0:T(8,128)(2,1)} %param.12) | copy-start | bytes 1769476
Sparse Core Ops, SparseCore 0:
  127.5 256.4 all-reduce.3
where the time goes:
time: 424 us; the launch traced here: 423 us
  waiting for transfers between devices  204 us (48%)
  blocking collectives  81.3 us (19%)
  matrix products  53.2 us (13%)
  local copies, waits for them, and re-layouts  30.7 us (7%)
  starting transfers between devices  18.9 us (4%)
  between operations  17.5 us (4%)
  other arithmetic  16.9 us (4%)
    psum x1, waiting for transfers between devices, shards(): lax.psum((in_raw, bin_raw, mid_raw, bmid_raw, out_raw), ('space', 'batch'))  171 us
    psum x1, blocking collectives, shards(): lax.psum((in_raw, bin_raw, mid_raw, bmid_raw, out_raw), ('space', 'batch'))  81.3 us
    all_to_all x1, waiting for transfers between devices, shards(): lax.all_to_all(wave_grad, 'space', split_axis=1, concat_axis=0, tiled=True)  33.3 us
    all_to_all x1, starting transfers between devices, shards(): lax.all_to_all(wave_grad, 'space', split_axis=1, concat_axis=0, tiled=True)  12.2 us
  transfers between devices with their start and end apart: 3, of which 2 were waited for; matrix products, arithmetic and copies ran while one was open for 9% of the time, Pallas kernels for 0%

commit v1 on v0

v1 whole, which is shorter than its diff:
```python
import functools
import math

import jax
import jax.numpy as jnp
import numpy as np
from jax import lax
from jax.experimental import pallas as pl
from jax.experimental.pallas import tpu as pltpu
from jax.sharding import PartitionSpec as P

MESH = pl.DeviceIdType.MESH
F32 = jnp.float32
BF16 = jnp.bfloat16

Z, X, NB = 8, 4, 8
SP = Z * X
TRAJ, WAVE, LATS = 2, 6, 8
CHAN, HIDDEN, LONS, DEG = 128, 256, 512, 192
COEF = 2 * DEG
MC = 2 * WAVE * SP
SEG = 40
ROWS = 32 * SEG
LIMIT = math.sqrt(2 * CHAN * HIDDEN + HIDDEN * HIDDEN + 2 * HIDDEN)


def fourier_rows():
    waves = WAVE * SP
    phase = (np.arange(waves)[:, None] * np.arange(LONS)[None, :]) % LONS
    phase = phase * (2.0 * math.pi / LONS)
    table = np.stack([np.cos(phase), -np.sin(phase)], axis=1) / math.sqrt(waves)
    return table.reshape(MC, LONS).astype(np.float32)


def dot(a, b, ca, cb):
    return lax.dot_general(a, b, (((ca,), (cb,)), ((), ())), preferred_element_type=F32)


def column(row_ref):
    return jnp.broadcast_to(row_ref[...], (128, row_ref.shape[1])).T


def gelu_pair(v):
    square = v * v
    tanh_part = jnp.tanh(v * (0.7978845608 + 0.7978845608 * 0.044715 * square))
    up = 0.5 + 0.5 * tanh_part
    value = v * up
    bend = 0.7978845608 + 0.7978845608 * 0.134145 * square
    slope = up + 0.5 * v * (1.0 - tanh_part * tanh_part) * bend
    return value, slope


def kernel(
    cot_hbm, grid_hbm, leg_hbm, inv_hbm, gw_ref, w_in, b_in, w_mid, b_mid, w_out, tab,
    out_hbm, g_in, g_bin, g_mid, g_bmid, g_out,
    cot, grid, leg, inv, out, bd, send1, recv1, send2, recv2, wide,
    h_in, h_mid, s_in, s_mid, w_in_t, w_mid_t, col_g, col_in, col_mid,
    acc, acc_bin, acc_bmid, got_a, got_z, total,
    in_sem, out_sem, s1_sem, r1_sem, s2_sem, r2_sem, sa_sem, ra_sem, sz_sem, rz_sem, sc_sem, rc_sem,
):
    me = lax.axis_index("space")
    bat = lax.axis_index("batch")
    z, x = me // X, me % X
    gi = bat * X + x

    loads = [
        pltpu.make_async_copy(inv_hbm, inv, in_sem.at[0]),
        pltpu.make_async_copy(leg_hbm, leg, in_sem.at[1]),
        pltpu.make_async_copy(cot_hbm.at[0], cot.at[0], in_sem.at[2]),
        pltpu.make_async_copy(cot_hbm.at[1], cot.at[1], in_sem.at[3]),
        pltpu.make_async_copy(grid_hbm, grid, in_sem.at[4]),
    ]
    for load in loads:
        load.start()

    def space_peer(s):
        return lax.rem(me + s, SP)

    def group_peer(s):
        g = lax.rem(gi + s, 32)
        return g, (z * X + g % X, g // X)

    def depth_peer(s):
        return lax.rem(z + s, Z) * X + x

    barrier = pltpu.get_barrier_semaphore()

    def greet(s, carry):
        pl.semaphore_signal(barrier, inc=1, device_id=(space_peer(s), bat), device_id_type=MESH)
        pl.semaphore_signal(barrier, inc=1, device_id=group_peer(s)[1], device_id_type=MESH)
        return carry

    lax.fori_loop(1, 32, greet, 0)

    def copy1(b, s):
        peer = space_peer(s)
        return pltpu.make_async_remote_copy(
            src_ref=send1.at[b, peer], dst_ref=recv1.at[b, me],
            send_sem=s1_sem.at[b, s], recv_sem=r1_sem.at[b, s],
            device_id=(peer, bat), device_id_type=MESH,
        )

    def copy2(b, s):
        peer = space_peer(s)
        return pltpu.make_async_remote_copy(
            src_ref=send2.at[b, peer], dst_ref=recv2.at[b, me],
            send_sem=s2_sem.at[b, s], recv_sem=r2_sem.at[b, s],
            device_id=(peer, bat), device_id_type=MESH,
        )

    def copy_a(s):
        g, where = group_peer(s)
        return pltpu.make_async_remote_copy(
            src_ref=acc.at[pl.ds(pl.multiple_of(g * SEG, 8), SEG)], dst_ref=got_a.at[gi],
            send_sem=sa_sem.at[s], recv_sem=ra_sem.at[s], device_id=where, device_id_type=MESH,
        )

    def copy_z(s):
        return pltpu.make_async_remote_copy(
            src_ref=got_z.at[z], dst_ref=got_z.at[z],
            send_sem=sz_sem.at[s], recv_sem=rz_sem.at[s],
            device_id=(depth_peer(s), bat), device_id_type=MESH,
        )

    def copy_c(s):
        _, where = group_peer(s)
        mine = pl.ds(pl.multiple_of(gi * SEG, 8), SEG)
        return pltpu.make_async_remote_copy(
            src_ref=total.at[mine], dst_ref=total.at[mine],
            send_sem=sc_sem.at[s], recv_sem=rc_sem.at[s], device_id=where, device_id_type=MESH,
        )

    def each(first, last, act):
        def body(s, carry):
            act(s)
            return carry

        lax.fori_loop(first, last, body, 0)

    col_g[...] = column(gw_ref)
    loads[0].wait()
    loads[1].wait()
    lane = lax.broadcasted_iota(jnp.int32, (DEG, 2 * COEF), 1)
    row = lax.broadcasted_iota(jnp.int32, (DEG, 2 * COEF), 0)
    pick = jnp.where((lane == row) | (lane == row + COEF + DEG), 1.0, 0.0).astype(BF16)
    lane = lax.broadcasted_iota(jnp.int32, (32, CHAN), 1)
    row = lax.broadcasted_iota(jnp.int32, (32, CHAN), 0)
    repeat = jnp.where(lane % 32 == row, 1.0, 0.0).astype(BF16)
    lane = lax.broadcasted_iota(jnp.int32, (CHAN, CHAN), 1)
    row = lax.broadcasted_iota(jnp.int32, (CHAN, CHAN), 0)
    same = lane // 32 == row // 32

    def spectral_in(b, m):
        block = inv[m].reshape(CHAN, 32)
        high = block.astype(BF16)
        low = (block - high.astype(F32)).astype(BF16)
        high = jnp.where(same, dot(high, repeat, 1, 0), 0.0).T.astype(BF16)
        low = jnp.where(same, dot(low, repeat, 1, 0), 0.0).T.astype(BF16)
        value = cot[b, m]
        value_high = value.astype(BF16)
        value_low = (value - value_high.astype(F32)).astype(BF16)
        grad = dot(
            jnp.concatenate([high, low, high], axis=1),
            jnp.concatenate([value_high, value_high, value_low], axis=0),
            1, 0,
        )
        out[b, m] = grad
        if b == 0:
            turned = dot(leg[m], pick, 0, 0).reshape(SP, LATS, 2 * COEF)
            both = jnp.concatenate([turned[:, :, :COEF], turned[:, :, COEF:]], axis=1)
            bd[m] = both.reshape(2 * LATS * SP, COEF).astype(BF16)
        sums = dot(bd[m], grad.astype(BF16), 1, 1).reshape(SP, 2, LATS, CHAN)
        scaled = sums * col_g[...].reshape(SP, 1, LATS, CHAN)
        send1[b, :, m] = scaled.reshape(SP, 2 * LATS, CHAN).astype(BF16)

    for b in range(TRAJ):
        loads[2 + b].wait()
        each(0, WAVE, functools.partial(spectral_in, b))
        if b == 0:
            pl.semaphore_wait(barrier, 62)
        each(1, SP, lambda s: copy1(b, s).start())
        recv1[b, me] = send1[b, me]

    w_in_t[...] = w_in[...].T
    w_mid_t[...] = w_mid[...].T
    col_in[...] = column(b_in)
    col_mid[...] = column(b_mid)
    acc[...] = jnp.zeros_like(acc)
    acc_bin[...] = jnp.zeros_like(acc_bin)
    acc_bmid[...] = jnp.zeros_like(acc_bmid)
    loads[4].wait()

    def forward(i):
        b, a = i // LATS, i % LATS
        pre = dot(w_in_t[...], grid[b, a], 1, 0)
        value, slope = gelu_pair(pre + jnp.concatenate([col_in[...]] * 4, axis=1))
        hidden = value.astype(BF16)
        h_in[i] = hidden
        s_in[i] = slope
        pre = dot(w_mid_t[...], hidden, 1, 0)
        value, slope = gelu_pair(pre + jnp.concatenate([col_mid[...]] * 4, axis=1))
        h_mid[i] = value.astype(BF16)
        s_mid[i] = slope

    each(0, TRAJ * LATS, forward)

    def lane_sum(v):
        return v[:, :128] + v[:, 128:256] + v[:, 256:384] + v[:, 384:]

    def backward(b, a):
        i = b * LATS + a
        part = wide[pl.ds(a, MC, stride=LATS), :].astype(BF16)
        tend = dot(part, tab[...], 0, 0).astype(BF16)
        acc[768:1024] += dot(h_mid[i], tend, 1, 1)
        err_mid = (dot(w_out[...], tend, 1, 0) * s_mid[i]).astype(BF16)
        mid = dot(h_in[i], err_mid, 1, 1)
        acc[256:512] += mid[:, :128]
        acc[512:768] += mid[:, 128:]
        acc_bmid[...] += lane_sum(err_mid.astype(F32))
        err_in = (dot(w_mid[...], err_mid, 1, 0) * s_in[i]).astype(BF16)
        raw = dot(grid[b, a], err_in, 1, 1)
        acc[0:128] += raw[:, :128]
        acc[128:256] += raw[:, 128:]
        acc_bin[...] += lane_sum(err_in.astype(F32))
        state = dot(w_in[...], err_in, 1, 0).astype(BF16)
        wide[pl.ds(a, MC, stride=LATS), :] = dot(tab[...], state, 1, 1)

    per_peer = 2 * WAVE * LATS

    def unpack(b, peer):
        rows = pl.ds(pl.multiple_of(peer * per_peer, per_peer), per_peer)
        wide[rows, :] = recv1[b, peer].reshape(per_peer, CHAN).astype(F32)

    def pack(b, peer):
        rows = pl.ds(pl.multiple_of(peer * per_peer, per_peer), per_peer)
        send2[b, peer] = wide[rows, :].astype(BF16).reshape(WAVE, 2 * LATS, CHAN)

    for b in range(TRAJ):
        unpack(b, me)

        def arrive(s):
            copy1(b, s).wait_recv()
            unpack(b, lax.rem(me + SP - s, SP))

        each(1, SP, arrive)
        each(0, LATS, functools.partial(backward, b))
        if b == TRAJ - 1:
            bins = jnp.sum(acc_bin[...].T, axis=0, keepdims=True)
            bmids = jnp.sum(acc_bmid[...].T, axis=0, keepdims=True)
            acc[1024:1025] = bins[:, :128]
            acc[1025:1026] = bins[:, 128:]
            acc[1026:1027] = bmids[:, :128]
            acc[1027:1028] = bmids[:, 128:]
            each(1, 32, lambda s: copy_a(s).start())

        def depart(s):
            pack(b, space_peer(s))
            copy2(b, s).start()

        each(1, SP, depart)
        pack(b, me)
        recv2[b, me] = send2[b, me]

    def spectral_out(b, m):
        back = recv2[b, :, m].reshape(2 * LATS * SP, CHAN)
        out[b, m] += dot(back, bd[m], 0, 0)
        pltpu.make_async_copy(out.at[b, m], out_hbm.at[b, m], out_sem.at[b, m]).start()

    def finish(b):
        each(1, SP, lambda s: copy2(b, s).wait_recv())
        each(0, WAVE, functools.partial(spectral_out, b))

    mine = pl.ds(pl.multiple_of(gi * SEG, 8), SEG)
    got_a[gi] = acc[mine]
    each(1, 32, lambda s: copy_a(s).wait_recv())
    got_z[z] = lax.fori_loop(1, 32, lambda i, t: t + got_a[i], got_a[0])
    each(1, Z, lambda s: copy_z(s).start())
    finish(0)
    each(1, Z, lambda s: copy_z(s).wait_recv())
    total[mine] = lax.fori_loop(1, Z, lambda i, t: t + got_z[i], got_z[0])
    each(1, 32, lambda s: copy_c(s).start())
    finish(1)
    each(1, 32, lambda s: copy_c(s).wait_recv())
    squares = total[...] * total[...]
    factor = jnp.minimum(F32(1.0), LIMIT / jnp.sqrt(jnp.sum(squares, keepdims=True) + 1e-06))
    g_in[:, :128] = factor * total[0:128]
    g_in[:, 128:] = factor * total[128:256]
    g_mid[:, :128] = factor * total[256:512]
    g_mid[:, 128:] = factor * total[512:768]
    g_out[...] = factor * total[768:1024]
    g_bin[:, :128] = factor * total[1024:1025]
    g_bin[:, 128:] = factor * total[1025:1026]
    g_bmid[:, :128] = factor * total[1026:1027]
    g_bmid[:, 128:] = factor * total[1027:1028]

    for b in range(TRAJ):
        each(1, SP, lambda s: copy1(b, s).wait_send())
        each(1, SP, lambda s: copy2(b, s).wait_send())
        each(0, WAVE, lambda m: pltpu.make_async_copy(
            out.at[b, m], out_hbm.at[b, m], out_sem.at[b, m]).wait())
    each(1, 32, lambda s: copy_a(s).wait_send())
    each(1, Z, lambda s: copy_z(s).wait_send())
    each(1, 32, lambda s: copy_c(s).wait_send())


def shards(
    cotangent, grid_state, legendre, inverse, gauss_weights, w_in, bias_in, w_mid, bias_mid, w_out
):
    table = jnp.asarray(fourier_rows(), F32).astype(BF16)
    vmem = pl.BlockSpec(memory_space=pltpu.VMEM)
    hbm = pl.BlockSpec(memory_space=pl.ANY)
    cols = TRAJ * LATS
    message = (TRAJ, SP, WAVE, 2 * LATS, CHAN)
    dma = pltpu.SemaphoreType.DMA
    outs = pl.pallas_call(
        kernel,
        out_shape=(
            jax.ShapeDtypeStruct((TRAJ, WAVE, CHAN, COEF), F32),
            jax.ShapeDtypeStruct((CHAN, HIDDEN), F32),
            jax.ShapeDtypeStruct((1, HIDDEN), F32),
            jax.ShapeDtypeStruct((HIDDEN, HIDDEN), F32),
            jax.ShapeDtypeStruct((1, HIDDEN), F32),
            jax.ShapeDtypeStruct((HIDDEN, CHAN), F32),
        ),
        in_specs=[hbm] * 4 + [vmem] * 7,
        out_specs=[hbm] + [vmem] * 5,
        scratch_shapes=[
            pltpu.VMEM((TRAJ, WAVE, CHAN, COEF), F32),
            pltpu.VMEM((TRAJ, LATS, CHAN, LONS), BF16),
            pltpu.VMEM((WAVE, DEG, LATS * SP), BF16),
            pltpu.VMEM((WAVE, 4, 32, 32), F32),
            pltpu.VMEM((TRAJ, WAVE, CHAN, COEF), F32),
            pltpu.VMEM((WAVE, 2 * LATS * SP, COEF), BF16),
            pltpu.VMEM(message, BF16),
            pltpu.VMEM(message, BF16),
            pltpu.VMEM(message, BF16),
            pltpu.VMEM(message, BF16),
            pltpu.VMEM((MC * LATS, CHAN), F32),
            pltpu.VMEM((cols, HIDDEN, LONS), BF16),
            pltpu.VMEM((cols, HIDDEN, LONS), BF16),
            pltpu.VMEM((cols, HIDDEN, LONS), F32),
            pltpu.VMEM((cols, HIDDEN, LONS), F32),
            pltpu.VMEM((HIDDEN, CHAN), BF16),
            pltpu.VMEM((HIDDEN, HIDDEN), BF16),
            pltpu.VMEM((LATS * SP, 128), F32),
            pltpu.VMEM((HIDDEN, 128), F32),
            pltpu.VMEM((HIDDEN, 128), F32),
            pltpu.VMEM((ROWS, 128), F32),
            pltpu.VMEM((HIDDEN, 128), F32),
            pltpu.VMEM((HIDDEN, 128), F32),
            pltpu.VMEM((32, SEG, 128), F32),
            pltpu.VMEM((Z, SEG, 128), F32),
            pltpu.VMEM((ROWS, 128), F32),
            dma((5,)),
            dma((TRAJ, WAVE)),
            dma((TRAJ, SP)),
            dma((TRAJ, SP)),
            dma((TRAJ, SP)),
            dma((TRAJ, SP)),
            dma((32,)),
            dma((32,)),
            dma((Z,)),
            dma((Z,)),
            dma((32,)),
            dma((32,)),
        ],
        compiler_params=pltpu.CompilerParams(
            collective_id=0, has_side_effects=True, vmem_limit_bytes=60 * 1024 * 1024
        ),
    )(
        cotangent, grid_state, legendre, inverse, gauss_weights.reshape(1, -1),
        w_in, bias_in.reshape(1, -1), w_mid, bias_mid.reshape(1, -1), w_out, table,
    )
    state, g_in, g_bin, g_mid, g_bmid, g_out = outs
    return state, g_in, g_bin.reshape(-1), g_mid, g_bmid.reshape(-1), g_out


def solution(mesh):
    return jax.shard_map(
        shards,
        mesh=mesh,
        in_specs=(
            P("batch", "space", None, None),
            P("batch", "space", None, None),
            P("space", None, None),
            P("space", None, None, None),
            P(),
            P(),
            P(),
            P(),
            P(),
            P(),
        ),
        out_specs=(P("batch", "space", None, None), P(), P(), P(), P(), P()),
        check_vma=False,
    )
```

time: 424 us -> 111 us (0.26)
  waiting for transfers between devices: 204 us -> 0 us
  Pallas kernels: 0 us -> 104 us
  blocking collectives: 81.3 us -> 0 us
  matrix products: 53.2 us -> 0 us
  local copies, waits for them, and re-layouts: 30.7 us -> 6.44 us
  starting transfers between devices: 18.9 us -> 0 us
  other arithmetic: 16.9 us -> 0 us
  between operations: 17.5 us -> 0.69 us
    psum x1 -> x0, waiting for transfers between devices: 171 us -> none  [shards(): lax.psum((in_raw, bin_raw, mid_raw, bmid_raw, out_raw), ('space', 'batch'))]
    pallas_call x0 -> x1, Pallas kernels: none -> 104 us  [shards(): pl.pallas_call(kernel, out_shape=(jax.ShapeDtypeStruct((TRAJ, WAVE, CHAN,...]
    psum x1 -> x0, blocking collectives: 81.3 us -> none  [shards(): lax.psum((in_raw, bin_raw, mid_raw, bmid_raw, out_raw), ('space', 'batch'))]
    dot_general x12 -> x0, matrix products: 53.2 us -> none  [the longest x1 7.59 us: shards(): jnp.einsum('hg,bago->baho', w_mid, err_mid, preferred_element_type=jnp.fl...]
    all_to_all x2 -> x0, waiting for transfers between devices: 33.3 us -> none  [the longest x1 33.3 us: shards(): lax.all_to_all(wave_grad, 'space', split_axis=1, concat_axis=0, tiled=True)]
    all_to_all x2 -> x0, starting transfers between devices: 18.9 us -> none  [the longest x1 12.2 us: shards(): lax.all_to_all(wave_grad, 'space', split_axis=1, concat_axis=0, tiled=True)]
    reshape x4 -> x0, local copies, waits for them, and re-layouts: 14.9 us -> none  [the longest x2 7.31 us: shards(): spectral = spectral.reshape(wave_dev, degrees, trajs, 2, channels)]
    reduce_sum x5 -> x0, other arithmetic: 5.9 us -> none  [the longest x2 2.14 us: shards(): total = total + jnp.sum(bmid_raw * bmid_raw) + jnp.sum(out_raw * out_raw)]
  transfers between devices with their start and end apart: 3 -> 0, of which waited for: 2 -> 0; matrix products, arithmetic and copies ran while one was open for 9% -> 0% of each run, Pallas kernels for 0% -> 0%
where the time goes in v1:
time: 111 us
  Pallas kernels  104 us (94%)
  local copies, waits for them, and re-layouts  6.44 us (6%)
    pallas_call x1, Pallas kernels, shards(): pl.pallas_call(kernel, out_shape=(jax.ShapeDtypeStruct((TRAJ, WAVE, CHAN,...  104 us
    unnamed x16, local copies, waits for them, and re-layouts  6.44 us

profile of v1, /device:TPU:1, one launch (start us, length us, event | category | flops | bytes accessed | tf_op | source)
XLA Modules:
  0.0 110.8 jit_solution(9975582370841956944)
XLA Ops:
  0.6 103.7 %shard_map.154 = (f32[2,6,128,384]{3,2,1,0:T(8,128)}, f32[128,256]{1,0:T(8,128)}, f32[1,256]{1,0:T(1,128)}, f32[256,256]{1,0:T(8,128)}, f32[1,256]{1,0:T(1,128)}, /*index=5*/f32[256,128]{1,0:T(8,128)}) custom-call(f32[2,6,128,384]{3,2,1,0:T(8,128)} %cot_hbm.1, bf16[2,8,128,512]{3,2,1,0:T(8,128)(2,1)} %grid_hbm.1, bf16[6,192,256]{2,1,0:T(8,128)(2,1)} %leg_hbm.1, ...), custom_call_target="tpu_custom_call" | custom-call | tf_op jit(solution)/shard_map/pallas_call | solution.py:315
  104.4 0.0 copy-start.2
  104.4 0.0 copy-start.4
  104.4 0.0 copy-start
  104.4 0.0 copy-start.3
  104.4 0.0 copy-start.1
  104.4 3.3 %copy.23 = f32[2,6,128,384]{3,2,1,0:T(8,128)} copy(f32[2,6,128,384]{3,2,1,0:T(8,128)} %get-tuple-element.24) | data formatting | bytes 4718592
  107.7 0.0 copy-done.2
  107.7 0.7 copy.24
  108.4 0.0 copy-done.4
  108.4 0.6 copy.25
  108.9 0.0 copy-done
  108.9 0.7 copy.26
  109.6 0.0 copy-done.3
  109.6 0.6 copy.27
  110.2 0.0 copy-done.1
  110.2 0.7 copy.28
Async XLA Ops:
  104.4 3.3 %copy-start.2 = (f32[128,256]{1,0:T(8,128)S(1)}, f32[128,256]{1,0:T(8,128)}, u32[]{:S(2)}) copy-start(f32[128,256]{1,0:T(8,128)} %get-tuple-element.25) | copy-start | bytes 393220
  104.4 4.0 %copy-start.4 = (f32[1,256]{1,0:T(1,128)S(1)}, f32[1,256]{1,0:T(1,128)}, u32[]{:S(2)}) copy-start(f32[1,256]{1,0:T(1,128)} %get-tuple-element.14) | copy-start | bytes 3076
  104.4 4.5 %copy-start = (f32[256,256]{1,0:T(8,128)S(1)}, f32[256,256]{1,0:T(8,128)}, u32[]{:S(2)}) copy-start(f32[256,256]{1,0:T(8,128)} %get-tuple-element.27) | copy-start | bytes 786436
  104.4 5.2 %copy-start.3 = (f32[1,256]{1,0:T(1,128)S(1)}, f32[1,256]{1,0:T(1,128)}, u32[]{:S(2)}) copy-start(f32[1,256]{1,0:T(1,128)} %get-tuple-element.16) | copy-start | bytes 3076
  104.4 5.8 %copy-start.1 = (f32[256,128]{1,0:T(8,128)S(1)}, f32[256,128]{1,0:T(8,128)}, u32[]{:S(2)}) copy-start(f32[256,128]{1,0:T(8,128)} %get-tuple-element.29) | copy-start | bytes 393220

commit v2 on v1

v2 whole, which is shorter than its diff:
```python
import functools
import math

import jax
import jax.numpy as jnp
import numpy as np
from jax import lax
from jax.experimental import pallas as pl
from jax.experimental.pallas import tpu as pltpu
from jax.sharding import PartitionSpec as P

MESH = pl.DeviceIdType.MESH
F32 = jnp.float32
BF16 = jnp.bfloat16

Z, X, NB = 8, 4, 8
SP = Z * X
TRAJ, WAVE, LATS = 2, 6, 8
CHAN, HIDDEN, LONS, DEG = 128, 256, 512, 192
COEF = 2 * DEG
MC = 2 * WAVE * SP
SEG = 40
ROWS = 32 * SEG
HELD = 16
LIMIT = math.sqrt(2 * CHAN * HIDDEN + HIDDEN * HIDDEN + 2 * HIDDEN)


def fourier_rows():
    waves = WAVE * SP
    phase = (np.arange(waves)[:, None] * np.arange(LONS)[None, :]) % LONS
    phase = phase * (2.0 * math.pi / LONS)
    table = np.stack([np.cos(phase), -np.sin(phase)], axis=1) / math.sqrt(waves)
    return table.reshape(MC, LONS).astype(np.float32)


def dot(a, b, ca, cb):
    return lax.dot_general(a, b, (((ca,), (cb,)), ((), ())), preferred_element_type=F32)


def column(row_ref):
    return jnp.broadcast_to(row_ref[...], (128, row_ref.shape[1])).T


def gelu_pair(v):
    square = v * v
    tanh_part = jnp.tanh(v * (0.7978845608 + 0.7978845608 * 0.044715 * square))
    up = 0.5 + 0.5 * tanh_part
    value = v * up
    bend = 0.7978845608 + 0.7978845608 * 0.134145 * square
    slope = up + 0.5 * v * (1.0 - tanh_part * tanh_part) * bend
    return value, slope


def legendre_back(back, leg):
    wide = back.astype(F32)
    real = wide[:, :LATS].reshape(LATS * SP, CHAN)
    imag = wide[:, LATS:].reshape(LATS * SP, CHAN)
    sums = dot(jnp.concatenate([real, imag], axis=1).astype(BF16), leg, 0, 1)
    return jnp.concatenate([sums[:CHAN], sums[CHAN:]], axis=1)


def kernel(
    cot_hbm, grid_hbm, leg_hbm, inv_hbm, gw_hbm, w_in_hbm, b_in_hbm, w_mid_hbm, b_mid_hbm, w_out_hbm,
    tab_hbm, done_hbm, spec_hbm, back_hbm, total,
    cot, grid, leg, inv, gw, w_in, b_in, w_mid, b_mid, w_out, tab,
    spec, solve, send1, recv1, send2, recv2, wide,
    h_in, h_mid, s_in, s_mid, w_in_t, w_mid_t, col_g, col_in, col_mid,
    acc, acc_bin, acc_bmid, got_a, got_z,
    in_sem, out_sem, own_sem,
    s1_sem, r1_sem, s2_sem, r2_sem, sa_sem, ra_sem, sz_sem, rz_sem, sc_sem, rc_sem,
):
    me = lax.axis_index("space")
    bat = lax.axis_index("batch")
    z, x = me // X, me % X
    gi = bat * X + x

    loads = [
        pltpu.make_async_copy(source, target, in_sem.at[i])
        for i, (source, target) in enumerate([
            (inv_hbm, inv), (cot_hbm.at[0], cot.at[0]), (leg_hbm, leg), (gw_hbm, gw),
            (cot_hbm.at[1], cot.at[1]), (w_in_hbm, w_in), (b_in_hbm, b_in), (w_mid_hbm, w_mid),
            (b_mid_hbm, b_mid), (grid_hbm, grid), (w_out_hbm, w_out), (tab_hbm, tab),
        ])
    ]
    for load in loads:
        load.start()

    def shift(t):
        i, g = t % 8, t // 8
        return 4 + (1 - 2 * (i % 2)) * ((i + 1) // 2), g + i // 2

    def space_peer(t):
        dz, dx = shift(t)
        return (z + dz) % Z * X + (x + dx) % X

    def space_source(t):
        dz, dx = shift(t)
        return (z - dz + Z) % Z * X + (x - dx + 2 * X) % X

    def group_peer(s):
        g = (gi + s) % 32
        return g, (z * X + g % X, g // X)

    def depth_peer(s):
        return (z + s) % Z * X + x

    def each(first, last, act, unroll=1):
        def body(s, carry):
            act(s)
            return carry

        lax.fori_loop(first, last, body, 0, unroll=unroll)

    def peers(act, first=0, last=31):
        each(first, last, lambda t: act(t + (t + 17) // 32))

    barrier = pltpu.get_barrier_semaphore()

    def greet(t):
        pl.semaphore_signal(barrier, inc=1, device_id=(space_peer(t), bat), device_id_type=MESH)

    def greet_group(s):
        pl.semaphore_signal(barrier, inc=1, device_id=group_peer(s)[1], device_id_type=MESH)

    peers(greet)
    each(1, 32, greet_group)

    def copy1(b, s):
        peer = space_peer(s)
        return pltpu.make_async_remote_copy(
            src_ref=send1.at[b, peer], dst_ref=recv1.at[b, me],
            send_sem=s1_sem.at[b], recv_sem=r1_sem.at[b],
            device_id=(peer, bat), device_id_type=MESH,
        )

    def copy2(b, s):
        peer = space_peer(s)
        return pltpu.make_async_remote_copy(
            src_ref=send2.at[b, peer], dst_ref=recv2.at[me] if b == 0 else back_hbm.at[me],
            send_sem=s2_sem.at[b], recv_sem=r2_sem.at[b],
            device_id=(peer, bat), device_id_type=MESH,
        )

    def copy_a(s):
        g, where = group_peer(s)
        return pltpu.make_async_remote_copy(
            src_ref=acc.at[pl.ds(pl.multiple_of(g * SEG, 8), SEG)], dst_ref=got_a.at[gi],
            send_sem=sa_sem, recv_sem=ra_sem, device_id=where, device_id_type=MESH,
        )

    def copy_z(s):
        return pltpu.make_async_remote_copy(
            src_ref=got_z.at[z], dst_ref=got_z.at[z],
            send_sem=sz_sem, recv_sem=rz_sem,
            device_id=(depth_peer(s), bat), device_id_type=MESH,
        )

    def copy_c(s):
        _, where = group_peer(s)
        mine = pl.ds(pl.multiple_of(gi * SEG, 8), SEG)
        return pltpu.make_async_remote_copy(
            src_ref=total.at[mine], dst_ref=total.at[mine],
            send_sem=sc_sem, recv_sem=rc_sem, device_id=where, device_id_type=MESH,
        )

    def bulk(source, target, send_sem, recv_sem):
        return pltpu.make_async_remote_copy(
            src_ref=source, dst_ref=target, send_sem=send_sem, recv_sem=recv_sem,
            device_id=(space_peer(0), bat), device_id_type=MESH,
        )

    def all1(b):
        part = pl.ds(0, SP - 1)
        return bulk(send1.at[b, part], recv1.at[b, part], s1_sem.at[b], r1_sem.at[b])

    def all2(b):
        part = pl.ds(0, SP - 1)
        target = recv2.at[part] if b == 0 else back_hbm.at[part]
        return bulk(send2.at[b, part], target, s2_sem.at[b], r2_sem.at[b])

    def all_a():
        return bulk(acc.at[pl.ds(0, 31 * SEG)], got_a.at[pl.ds(0, 31)], sa_sem, ra_sem)

    def all_z():
        return bulk(got_z.at[pl.ds(0, Z - 1)], got_z.at[pl.ds(0, Z - 1)], sz_sem, rz_sem)

    def all_c():
        part = pl.ds(0, 31 * SEG)
        return bulk(total.at[part], total.at[part], sc_sem, rc_sem)

    lane = lax.broadcasted_iota(jnp.int32, (32, CHAN), 1)
    row = lax.broadcasted_iota(jnp.int32, (32, CHAN), 0)
    repeat = jnp.where(lane % 32 == row, 1.0, 0.0).astype(BF16)
    lane = lax.broadcasted_iota(jnp.int32, (CHAN, CHAN), 1)
    row = lax.broadcasted_iota(jnp.int32, (CHAN, CHAN), 0)
    same = lane // 32 == row // 32

    def spectral_in(b, m):
        if b == 0:
            block = inv[m].reshape(CHAN, 32)
            high = block.astype(BF16)
            low = (block - high.astype(F32)).astype(BF16)
            high = jnp.where(same, dot(high, repeat, 1, 0), 0.0).T.astype(BF16)
            low = jnp.where(same, dot(low, repeat, 1, 0), 0.0).T.astype(BF16)
            solve[m] = jnp.concatenate([high, low, high], axis=1)
        value = cot[b, m]
        value_high = value.astype(BF16)
        value_low = (value - value_high.astype(F32)).astype(BF16)
        grad = dot(
            solve[m], jnp.concatenate([value_high, value_high, value_low], axis=0), 1, 0
        )
        spec[b, m] = grad
        half = grad.astype(BF16)
        half = jnp.concatenate([half[:, :DEG], half[:, DEG:]], axis=0)
        sums = dot(leg[m], half, 0, 1)
        scaled = (sums * jnp.concatenate([col_g[...]] * 2, axis=1)).reshape(SP, LATS, 2 * CHAN)
        scaled = jnp.concatenate([scaled[:, :, :CHAN], scaled[:, :, CHAN:]], axis=1)
        send1[b, :, m] = scaled.astype(BF16)
        if b == 1:
            pltpu.make_async_copy(spec.at[1, m], spec_hbm.at[m], out_sem.at[1, m]).start()

    for load in loads[:4]:
        load.wait()
    col_g[...] = column(gw)
    for b in range(TRAJ):
        if b == 1:
            loads[4].wait()
        for m in range(WAVE):
            spectral_in(b, m)
        if b == 0:
            pl.semaphore_wait(barrier, 62)
        peers(lambda t: copy1(b, t).start())
        recv1[b, me] = send1[b, me]

    for load in loads[5:]:
        load.wait()
    w_in_t[...] = w_in[...].T
    w_mid_t[...] = w_mid[...].T
    col_in[...] = column(b_in)
    col_mid[...] = column(b_mid)
    acc[...] = jnp.zeros_like(acc)
    acc_bin[...] = jnp.zeros_like(acc_bin)
    acc_bmid[...] = jnp.zeros_like(acc_bmid)
    def forward(i):
        b, a = i // LATS, i % LATS
        pre = dot(w_in_t[...], grid[b, a], 1, 0)
        value, slope = gelu_pair(pre + jnp.concatenate([col_in[...]] * 4, axis=1))
        hidden = value.astype(BF16)
        h_in[i] = hidden
        s_in[i] = slope
        pre = dot(w_mid_t[...], hidden, 1, 0)
        value, slope = gelu_pair(pre + jnp.concatenate([col_mid[...]] * 4, axis=1))
        h_mid[i] = value.astype(BF16)
        s_mid[i] = slope

    each(0, TRAJ * LATS, forward)

    def lane_sum(v):
        return v[:, :128] + v[:, 128:256] + v[:, 256:384] + v[:, 384:]

    def backward(b, a):
        i = b * LATS + a
        part = wide[pl.ds(a, MC, stride=LATS), :].astype(BF16)
        tend = dot(part, tab[...], 0, 0).astype(BF16)
        acc[768:1024] += dot(h_mid[i], tend, 1, 1)
        err_mid = (dot(w_out[...], tend, 1, 0) * s_mid[i]).astype(BF16)
        mid = dot(h_in[i], err_mid, 1, 1)
        acc[256:512] += mid[:, :128]
        acc[512:768] += mid[:, 128:]
        acc_bmid[...] += lane_sum(err_mid.astype(F32))
        err_in = (dot(w_mid[...], err_mid, 1, 0) * s_in[i]).astype(BF16)
        raw = dot(grid[b, a], err_in, 1, 1)
        acc[0:128] += raw[:, :128]
        acc[128:256] += raw[:, 128:]
        acc_bin[...] += lane_sum(err_in.astype(F32))
        state = dot(w_in[...], err_in, 1, 0).astype(BF16)
        wide[pl.ds(a, MC, stride=LATS), :] = dot(tab[...], state, 1, 1)

    per_peer = 2 * WAVE * LATS

    def unpack(b, peer):
        rows = pl.ds(pl.multiple_of(peer * per_peer, per_peer), per_peer)
        wide[rows, :] = recv1[b, peer].reshape(per_peer, CHAN).astype(F32)

    def pack(b, peer):
        rows = pl.ds(pl.multiple_of(peer * per_peer, per_peer), per_peer)
        send2[b, peer] = wide[rows, :].astype(BF16).reshape(WAVE, 2 * LATS, CHAN)

    for b in range(TRAJ):
        all1(b).wait_recv()
        each(0, SP, functools.partial(unpack, b), 4)
        each(0, LATS, functools.partial(backward, b), 2)

        def depart(t):
            pack(b, space_peer(t))
            copy2(b, t).start()

        if b == 0:
            peers(depart)
            pack(b, me)
            recv2[me] = send2[b, me]

    bins = jnp.sum(acc_bin[...].T, axis=0, keepdims=True)
    bmids = jnp.sum(acc_bmid[...].T, axis=0, keepdims=True)
    acc[1024:1025] = bins[:, :128]
    acc[1025:1026] = bins[:, 128:]
    acc[1026:1027] = bmids[:, :128]
    acc[1027:1028] = bmids[:, 128:]
    each(1, 32, lambda s: copy_a(s).start())
    peers(depart, 0, HELD)
    pack(1, me)
    own = pltpu.make_async_copy(send2.at[1, me], back_hbm.at[me], own_sem)
    own.start()
    mine = pl.ds(pl.multiple_of(gi * SEG, 8), SEG)
    got_a[gi] = acc[mine]
    all_a().wait_recv()
    got_z[z] = lax.fori_loop(1, 32, lambda i, t: t + got_a[i], got_a[0])
    each(1, Z, lambda s: copy_z(s).start())
    peers(depart, HELD, 31)

    def finish(m):
        spec[0, m] += legendre_back(recv2[:, m], leg[m])
        pltpu.make_async_copy(spec.at[0, m], done_hbm.at[m], out_sem.at[0, m]).start()

    all2(0).wait_recv()
    for m in range(WAVE):
        finish(m)
    all_z().wait_recv()
    total[mine] = lax.fori_loop(1, Z, lambda i, t: t + got_z[i], got_z[0])
    each(1, 32, lambda s: copy_c(s).start())
    own.wait()
    for b in range(TRAJ):
        all1(b).wait_send()
        all2(b).wait_send()
    for m in range(WAVE):
        pltpu.make_async_copy(spec.at[0, m], done_hbm.at[m], out_sem.at[0, m]).wait()
        pltpu.make_async_copy(spec.at[1, m], spec_hbm.at[m], out_sem.at[1, m]).wait()
    all_a().wait_send()
    all_z().wait_send()
    all_c().wait_recv()
    all_c().wait_send()
    all2(1).wait_recv()


def last_kernel(
    done_hbm, spec_hbm, back_hbm, leg_hbm, total_hbm,
    out_hbm, g_in, g_bin, g_mid, g_bmid, g_out,
    held, spec, back, leg, total, sem, out_sem, done_sem, total_sem,
):
    done = pltpu.make_async_copy(done_hbm, held, done_sem.at[0])
    store = pltpu.make_async_copy(held, out_hbm.at[0], done_sem.at[1])
    loads = [
        [
            pltpu.make_async_copy(back_hbm.at[:, m], back.at[:, m], sem.at[m, 0]),
            pltpu.make_async_copy(leg_hbm.at[m], leg.at[m], sem.at[m, 1]),
            pltpu.make_async_copy(spec_hbm.at[m], spec.at[m], sem.at[m, 2]),
        ]
        for m in range(WAVE)
    ]
    sums = pltpu.make_async_copy(total_hbm, total, total_sem)
    for load in loads[0]:
        load.start()
    done.start()
    for load in sum(loads[1:], []):
        load.start()
    sums.start()
    stores = [store]
    for m in range(WAVE):
        for load in loads[m]:
            load.wait()
        spec[m] += legendre_back(back[:, m], leg[m])
        stores.append(pltpu.make_async_copy(spec.at[m], out_hbm.at[1, m], out_sem.at[m]))
        stores[-1].start()
        if m == 0:
            done.wait()
            store.start()
    sums.wait()
    squares = total[...] * total[...]
    factor = jnp.minimum(F32(1.0), LIMIT / jnp.sqrt(jnp.sum(squares, keepdims=True) + 1e-06))
    g_in[:, :128] = factor * total[0:128]
    g_in[:, 128:] = factor * total[128:256]
    g_mid[:, :128] = factor * total[256:512]
    g_mid[:, 128:] = factor * total[512:768]
    g_out[...] = factor * total[768:1024]
    g_bin[:, :128] = factor * total[1024:1025]
    g_bin[:, 128:] = factor * total[1025:1026]
    g_bmid[:, :128] = factor * total[1026:1027]
    g_bmid[:, 128:] = factor * total[1027:1028]
    for store in stores:
        store.wait()


def shards(
    cotangent, grid_state, legendre, inverse, gauss_weights, w_in, bias_in, w_mid, bias_mid, w_out
):
    table = jnp.asarray(fourier_rows(), F32).astype(BF16)
    vmem = pl.BlockSpec(memory_space=pltpu.VMEM)
    hbm = pl.BlockSpec(memory_space=pl.ANY)
    cols = TRAJ * LATS
    message = (TRAJ, SP, WAVE, 2 * LATS, CHAN)
    dma = pltpu.SemaphoreType.DMA
    state_half = jax.ShapeDtypeStruct((WAVE, CHAN, COEF), F32)
    done, spec, back, total = pl.pallas_call(
        kernel,
        name="exchange",
        out_shape=(
            state_half,
            state_half,
            jax.ShapeDtypeStruct(message[1:], BF16),
            jax.ShapeDtypeStruct((ROWS, 128), F32),
        ),
        in_specs=[hbm] * 11,
        out_specs=[hbm] * 3 + [vmem],
        scratch_shapes=[
            pltpu.VMEM((TRAJ, WAVE, CHAN, COEF), F32),
            pltpu.VMEM((TRAJ, LATS, CHAN, LONS), BF16),
            pltpu.VMEM((WAVE, DEG, LATS * SP), BF16),
            pltpu.VMEM((WAVE, 4, 32, 32), F32),
            pltpu.VMEM((1, LATS * SP), F32),
            pltpu.VMEM((CHAN, HIDDEN), BF16),
            pltpu.VMEM((1, HIDDEN), F32),
            pltpu.VMEM((HIDDEN, HIDDEN), BF16),
            pltpu.VMEM((1, HIDDEN), F32),
            pltpu.VMEM((HIDDEN, CHAN), BF16),
            pltpu.VMEM((MC, LONS), BF16),
            pltpu.VMEM((TRAJ, WAVE, CHAN, COEF), F32),
            pltpu.VMEM((WAVE, CHAN, 3 * CHAN), BF16),
            pltpu.VMEM(message, BF16),
            pltpu.VMEM(message, BF16),
            pltpu.VMEM(message, BF16),
            pltpu.VMEM(message[1:], BF16),
            pltpu.VMEM((MC * LATS, CHAN), F32),
            pltpu.VMEM((cols, HIDDEN, LONS), BF16),
            pltpu.VMEM((cols, HIDDEN, LONS), BF16),
            pltpu.VMEM((cols, HIDDEN, LONS), F32),
            pltpu.VMEM((cols, HIDDEN, LONS), F32),
            pltpu.VMEM((HIDDEN, CHAN), BF16),
            pltpu.VMEM((HIDDEN, HIDDEN), BF16),
            pltpu.VMEM((LATS * SP, 128), F32),
            pltpu.VMEM((HIDDEN, 128), F32),
            pltpu.VMEM((HIDDEN, 128), F32),
            pltpu.VMEM((ROWS, 128), F32),
            pltpu.VMEM((HIDDEN, 128), F32),
            pltpu.VMEM((HIDDEN, 128), F32),
            pltpu.VMEM((32, SEG, 128), F32),
            pltpu.VMEM((Z, SEG, 128), F32),
            dma((12,)),
            dma((TRAJ, WAVE)),
            dma,
            dma((TRAJ,)),
            dma((TRAJ,)),
            dma((TRAJ,)),
            dma((TRAJ,)),
            dma,
            dma,
            dma,
            dma,
            dma,
            dma,
        ],
        compiler_params=pltpu.CompilerParams(
            collective_id=0, has_side_effects=True, vmem_limit_bytes=60 * 1024 * 1024
        ),
    )(
        cotangent, grid_state, legendre, inverse, gauss_weights.reshape(1, -1),
        w_in, bias_in.reshape(1, -1), w_mid, bias_mid.reshape(1, -1), w_out, table,
    )
    state, g_in, g_bin, g_mid, g_bmid, g_out = pl.pallas_call(
        last_kernel,
        name="finish",
        out_shape=(
            jax.ShapeDtypeStruct((TRAJ, WAVE, CHAN, COEF), F32),
            jax.ShapeDtypeStruct((CHAN, HIDDEN), F32),
            jax.ShapeDtypeStruct((1, HIDDEN), F32),
            jax.ShapeDtypeStruct((HIDDEN, HIDDEN), F32),
            jax.ShapeDtypeStruct((1, HIDDEN), F32),
            jax.ShapeDtypeStruct((HIDDEN, CHAN), F32),
        ),
        in_specs=[hbm] * 5,
        out_specs=[hbm] + [vmem] * 5,
        scratch_shapes=[
            pltpu.VMEM((WAVE, CHAN, COEF), F32),
            pltpu.VMEM((WAVE, CHAN, COEF), F32),
            pltpu.VMEM(message[1:], BF16),
            pltpu.VMEM((WAVE, DEG, LATS * SP), BF16),
            pltpu.VMEM((ROWS, 128), F32),
            dma((WAVE, 3)),
            dma((WAVE,)),
            dma((2,)),
            dma,
        ],
        compiler_params=pltpu.CompilerParams(vmem_limit_bytes=60 * 1024 * 1024),
    )(done, spec, back, legendre, total)
    return state, g_in, g_bin.reshape(-1), g_mid, g_bmid.reshape(-1), g_out


def solution(mesh):
    return jax.shard_map(
        shards,
        mesh=mesh,
        in_specs=(
            P("batch", "space", None, None),
            P("batch", "space", None, None),
            P("space", None, None),
            P("space", None, None, None),
            P(),
            P(),
            P(),
            P(),
            P(),
            P(),
        ),
        out_specs=(P("batch", "space", None, None), P(), P(), P(), P(), P()),
        check_vma=False,
    )
```

time: 111 us -> 99.3 us (0.89)
  local copies, waits for them, and re-layouts: 6.44 us -> 0 us
  Pallas kernels: 104 us -> 98.6 us
    unnamed x16 -> x0, local copies, waits for them, and re-layouts: 6.44 us -> none
    pallas_call x1 -> x2, Pallas kernels: 104 us -> 98.6 us  [the longest x1 93.2 us: shards(): pl.pallas_call(kernel, name='exchange', out_shape=(state_half, state_half...]
where the time goes in v2:
time: 99.3 us; the launch traced here: 99.2 us
  Pallas kernels  98.6 us (99%)
    pallas_call x1, Pallas kernels, shards(): pl.pallas_call(kernel, name='exchange', out_shape=(state_half, state_half...  93.2 us
    pallas_call x1, Pallas kernels, shards(): pl.pallas_call(last_kernel, name='finish', out_shape=(jax.ShapeDtypeStruc...  5.39 us

profile of v2, /device:TPU:1, one launch (start us, length us, event | category | flops | bytes accessed | tf_op | source)
XLA Modules:
  0.0 99.2 jit_solution(2790408740609452408)
XLA Ops:
  0.6 93.2 %exchange.1 = (f32[6,128,384]{2,1,0:T(8,128)}, f32[6,128,384]{2,1,0:T(8,128)}, bf16[32,6,16,128]{3,2,1,0:T(8,128)(2,1)}, f32[1280,128]{1,0:T(8,128)}) custom-call(f32[2,6,128,384]{3,2,1,0:T(8,128)} %cot_hbm.1, bf16[2,8,128,512]{3,2,1,0:T(8,128)(2,1)} %grid_hbm.1, bf16[6,192,256]{2,1,0:T(8,128)(2,1)} %leg_hbm.3, f32[6,4,32,32]{3,2,1,0:T(8,128)} %inv_hbm.1, ...), custom_call_target="tpu_custom_call" | custom-call | tf_op jit(solution)/shard_map/exchange/pallas_call | solution.py:403
  93.8 5.4 %finish.1 = (f32[2,6,128,384]{3,2,1,0:T(8,128)}, f32[128,256]{1,0:T(8,128)}, f32[1,256]{1,0:T(1,128)}, f32[256,256]{1,0:T(8,128)}, f32[1,256]{1,0:T(1,128)}, /*index=5*/f32[256,128]{1,0:T(8,128)}) custom-call(f32[6,128,384]{2,1,0:T(8,128)} %get-tuple-element.16.done_hbm, f32[6,128,384]{2,1,0:T(8,128)} %get-tuple-element.17.spec_hbm, ...), custom_call_target="tpu_custom_call" | custom-call | tf_op jit(solution)/shard_map/finish/pallas_call | solution.py:468

commit v3 on v2

--- a/solution.py
+++ b/solution.py
@@ -16,10 +16,11 @@
 Z, X, NB = 8, 4, 8
 SP = Z * X
 TRAJ, WAVE, LATS = 2, 6, 8
+HALF = LATS // 2
 CHAN, HIDDEN, LONS, DEG = 128, 256, 512, 192
 COEF = 2 * DEG
 MC = 2 * WAVE * SP
-SEG = 40
+SEG = 48
 ROWS = 32 * SEG
 HELD = 16
 LIMIT = math.sqrt(2 * CHAN * HIDDEN + HIDDEN * HIDDEN + 2 * HIDDEN)
@@ -51,12 +52,22 @@
     return value, slope
 
 
-def legendre_back(back, leg):
-    wide = back.astype(F32)
-    real = wide[:, :LATS].reshape(LATS * SP, CHAN)
-    imag = wide[:, LATS:].reshape(LATS * SP, CHAN)
-    sums = dot(jnp.concatenate([real, imag], axis=1).astype(BF16), leg, 0, 1)
+def swap_halves(a, b):
+    first = lax.broadcasted_iota(jnp.int32, a.shape, 1) < 4
+    return jnp.where(first, a, pltpu.roll(b, 4, 1)), jnp.where(first, pltpu.roll(a, 4, 1), b)
+
+
+def legendre_back(low, high, leg):
+    real, imag = swap_halves(low, high)
+    both = jnp.concatenate([real, imag], axis=2).reshape(LATS * SP, 2 * CHAN)
+    sums = dot(both.astype(BF16), leg, 0, 1)
     return jnp.concatenate([sums[:CHAN], sums[CHAN:]], axis=1)
+
+
+def sum_of(ref, count):
+    first = ref[0].astype(F32)
+    whole = lax.fori_loop(1, count, lambda i, t: t + ref[i].astype(F32), first)
+    return whole.astype(BF16)
 
 
 def kernel(
@@ -65,7 +76,7 @@
     cot, grid, leg, inv, gw, w_in, b_in, w_mid, b_mid, w_out, tab,
     spec, solve, send1, recv1, send2, recv2, wide,
     h_in, h_mid, s_in, s_mid, w_in_t, w_mid_t, col_g, col_in, col_mid,
-    acc, acc_bin, acc_bmid, got_a, got_z,
+    acc, acc_bin, acc_bmid, parts, got_a, got_z,
     in_sem, out_sem, own_sem,
     s1_sem, r1_sem, s2_sem, r2_sem, sa_sem, ra_sem, sz_sem, rz_sem, sc_sem, rc_sem,
 ):
@@ -93,10 +104,6 @@
         dz, dx = shift(t)
         return (z + dz) % Z * X + (x + dx) % X
 
-    def space_source(t):
-        dz, dx = shift(t)
-        return (z - dz + Z) % Z * X + (x - dx + 2 * X) % X
-
     def group_peer(s):
         g = (gi + s) % 32
         return g, (z * X + g % X, g // X)
@@ -125,26 +132,27 @@
     peers(greet)
     each(1, 32, greet_group)
 
-    def copy1(b, s):
+    def copy1(q, s):
         peer = space_peer(s)
         return pltpu.make_async_remote_copy(
-            src_ref=send1.at[b, peer], dst_ref=recv1.at[b, me],
-            send_sem=s1_sem.at[b], recv_sem=r1_sem.at[b],
+            src_ref=send1.at[q, peer], dst_ref=recv1.at[q, me],
+            send_sem=s1_sem.at[q], recv_sem=r1_sem.at[q],
             device_id=(peer, bat), device_id_type=MESH,
         )
 
-    def copy2(b, s):
+    def copy2(q, s):
         peer = space_peer(s)
         return pltpu.make_async_remote_copy(
-            src_ref=send2.at[b, peer], dst_ref=recv2.at[me] if b == 0 else back_hbm.at[me],
-            send_sem=s2_sem.at[b], recv_sem=r2_sem.at[b],
+            src_ref=send2.at[q, peer],
+            dst_ref=recv2.at[q, me] if q < 2 else back_hbm.at[q - 2, me],
+            send_sem=s2_sem.at[q], recv_sem=r2_sem.at[q],
             device_id=(peer, bat), device_id_type=MESH,
         )
 
     def copy_a(s):
         g, where = group_peer(s)
         return pltpu.make_async_remote_copy(
-            src_ref=acc.at[pl.ds(pl.multiple_of(g * SEG, 8), SEG)], dst_ref=got_a.at[gi],
+            src_ref=parts.at[pl.ds(pl.multiple_of(g * SEG, SEG), SEG)], dst_ref=got_a.at[gi],
             send_sem=sa_sem, recv_sem=ra_sem, device_id=where, device_id_type=MESH,
         )
 
@@ -157,7 +165,7 @@
 
     def copy_c(s):
         _, where = group_peer(s)
-        mine = pl.ds(pl.multiple_of(gi * SEG, 8), SEG)
+        mine = pl.ds(pl.multiple_of(gi * SEG, SEG), SEG)
         return pltpu.make_async_remote_copy(
             src_ref=total.at[mine], dst_ref=total.at[mine],
             send_sem=sc_sem, recv_sem=rc_sem, device_id=where, device_id_type=MESH,
@@ -169,17 +177,17 @@
             device_id=(space_peer(0), bat), device_id_type=MESH,
         )
 
-    def all1(b):
+    def all1(q):
         part = pl.ds(0, SP - 1)
-        return bulk(send1.at[b, part], recv1.at[b, part], s1_sem.at[b], r1_sem.at[b])
-
-    def all2(b):
+        return bulk(send1.at[q, part], recv1.at[q, part], s1_sem.at[q], r1_sem.at[q])
+
+    def all2(q):
         part = pl.ds(0, SP - 1)
-        target = recv2.at[part] if b == 0 else back_hbm.at[part]
-        return bulk(send2.at[b, part], target, s2_sem.at[b], r2_sem.at[b])
+        target = recv2.at[q, part] if q < 2 else back_hbm.at[q - 2, part]
+        return bulk(send2.at[q, part], target, s2_sem.at[q], r2_sem.at[q])
 
     def all_a():
-        return bulk(acc.at[pl.ds(0, 31 * SEG)], got_a.at[pl.ds(0, 31)], sa_sem, ra_sem)
+        return bulk(parts.at[pl.ds(0, 31 * SEG)], got_a.at[pl.ds(0, 31)], sa_sem, ra_sem)
 
     def all_z():
         return bulk(got_z.at[pl.ds(0, Z - 1)], got_z.at[pl.ds(0, Z - 1)], sz_sem, rz_sem)
@@ -214,10 +222,9 @@
         half = jnp.concatenate([half[:, :DEG], half[:, DEG:]], axis=0)
         sums = dot(leg[m], half, 0, 1)
         scaled = (sums * jnp.concatenate([col_g[...]] * 2, axis=1)).reshape(SP, LATS, 2 * CHAN)
-        scaled = jnp.concatenate([scaled[:, :, :CHAN], scaled[:, :, CHAN:]], axis=1)
-        send1[b, :, m] = scaled.astype(BF16)
         if b == 1:
             pltpu.make_async_copy(spec.at[1, m], spec_hbm.at[m], out_sem.at[1, m]).start()
+        return swap_halves(scaled[:, :, :CHAN], scaled[:, :, CHAN:])
 
     for load in loads[:4]:
         load.wait()
@@ -225,12 +232,16 @@
     for b in range(TRAJ):
         if b == 1:
             loads[4].wait()
-        for m in range(WAVE):
-            spectral_in(b, m)
+        for m in range(0, WAVE, 2):
+            for h, pair in enumerate(zip(spectral_in(b, m), spectral_in(b, m + 1), strict=True)):
+                send1[2 * b + h, :, 8 * m : 8 * m + 16] = jnp.concatenate(pair, axis=1).astype(BF16)
         if b == 0:
             pl.semaphore_wait(barrier, 62)
-        peers(lambda t: copy1(b, t).start())
-        recv1[b, me] = send1[b, me]
+        if b == 0:
+            peers(lambda t: copy1(0, t).start())
+            peers(lambda t: copy1(1, t).start())
+        for q in (2 * b, 2 * b + 1):
+            recv1[q, me] = send1[q, me]
 
     for load in loads[5:]:
         load.wait()
@@ -243,6 +254,16 @@
     acc_bmid[...] = jnp.zeros_like(acc_bmid)
     def forward(i):
         b, a = i // LATS, i % LATS
+        first = 4 * (i % 8)
+
+        @pl.when(i < 8)
+        def _():
+            peers(lambda t: copy1(2, t).start(), first, jnp.minimum(first + 4, 31))
+
+        @pl.when(i >= 8)
+        def _():
+            peers(lambda t: copy1(3, t).start(), first, jnp.minimum(first + 4, 31))
+
         pre = dot(w_in_t[...], grid[b, a], 1, 0)
         value, slope = gelu_pair(pre + jnp.concatenate([col_in[...]] * 4, axis=1))
         hidden = value.astype(BF16)
@@ -258,9 +279,10 @@
     def lane_sum(v):
         return v[:, :128] + v[:, 128:256] + v[:, 256:384] + v[:, 384:]
 
-    def backward(b, a):
-        i = b * LATS + a
-        part = wide[pl.ds(a, MC, stride=LATS), :].astype(BF16)
+    def backward(q, a):
+        i = q * HALF + a
+        rows = pl.ds(a, MC, stride=HALF)
+        part = wide[rows, :].astype(BF16)
         tend = dot(part, tab[...], 0, 0).astype(BF16)
         acc[768:1024] += dot(h_mid[i], tend, 1, 1)
         err_mid = (dot(w_out[...], tend, 1, 0) * s_mid[i]).astype(BF16)
@@ -269,36 +291,36 @@
         acc[512:768] += mid[:, 128:]
         acc_bmid[...] += lane_sum(err_mid.astype(F32))
         err_in = (dot(w_mid[...], err_mid, 1, 0) * s_in[i]).astype(BF16)
-        raw = dot(grid[b, a], err_in, 1, 1)
+        raw = dot(grid[q // 2, q % 2 * HALF + a], err_in, 1, 1)
         acc[0:128] += raw[:, :128]
         acc[128:256] += raw[:, 128:]
         acc_bin[...] += lane_sum(err_in.astype(F32))
         state = dot(w_in[...], err_in, 1, 0).astype(BF16)
-        wide[pl.ds(a, MC, stride=LATS), :] = dot(tab[...], state, 1, 1)
-
-    per_peer = 2 * WAVE * LATS
-
-    def unpack(b, peer):
+        wide[rows, :] = dot(tab[...], state, 1, 1)
+
+    per_peer = 2 * WAVE * HALF
+
+    def unpack(q, peer):
         rows = pl.ds(pl.multiple_of(peer * per_peer, per_peer), per_peer)
-        wide[rows, :] = recv1[b, peer].reshape(per_peer, CHAN).astype(F32)
-
-    def pack(b, peer):
+        wide[rows, :] = recv1[q, peer].astype(F32)
+
+    def pack(q, peer):
         rows = pl.ds(pl.multiple_of(peer * per_peer, per_peer), per_peer)
-        send2[b, peer] = wide[rows, :].astype(BF16).reshape(WAVE, 2 * LATS, CHAN)
-
-    for b in range(TRAJ):
-        all1(b).wait_recv()
-        each(0, SP, functools.partial(unpack, b), 4)
-        each(0, LATS, functools.partial(backward, b), 2)
-
-        def depart(t):
-            pack(b, space_peer(t))
-            copy2(b, t).start()
-
-        if b == 0:
-            peers(depart)
-            pack(b, me)
-            recv2[me] = send2[b, me]
+        send2[q, peer] = wide[rows, :].astype(BF16)
+
+    def depart(q, t):
+        pack(q, space_peer(t))
+        copy2(q, t).start()
+
+    for q in range(2 * TRAJ):
+        all1(q).wait_recv()
+        each(0, SP, functools.partial(unpack, q), 4)
+        each(0, HALF, functools.partial(backward, q), HALF)
+        if q < 3:
+            peers(functools.partial(depart, q))
+            pack(q, me)
+            if q < 2:
+                recv2[q, me] = send2[q, me]
 
     bins = jnp.sum(acc_bin[...].T, axis=0, keepdims=True)
     bmids = jnp.sum(acc_bmid[...].T, axis=0, keepdims=True)
@@ -306,32 +328,34 @@
     acc[1025:1026] = bins[:, 128:]
     acc[1026:1027] = bmids[:, :128]
     acc[1027:1028] = bmids[:, 128:]
+    parts[...] = acc[...].astype(BF16)
     each(1, 32, lambda s: copy_a(s).start())
-    peers(depart, 0, HELD)
-    pack(1, me)
-    own = pltpu.make_async_copy(send2.at[1, me], back_hbm.at[me], own_sem)
+    peers(functools.partial(depart, 3), 0, HELD)
+    pack(3, me)
+    own = pltpu.make_async_copy(send2.at[pl.ds(2, 2), me], back_hbm.at[:, me], own_sem)
     own.start()
-    mine = pl.ds(pl.multiple_of(gi * SEG, 8), SEG)
-    got_a[gi] = acc[mine]
+    mine = pl.ds(pl.multiple_of(gi * SEG, SEG), SEG)
+    got_a[gi] = parts[mine]
     all_a().wait_recv()
-    got_z[z] = lax.fori_loop(1, 32, lambda i, t: t + got_a[i], got_a[0])
+    got_z[z] = sum_of(got_a, 32)
     each(1, Z, lambda s: copy_z(s).start())
-    peers(depart, HELD, 31)
-
-    def finish(m):
-        spec[0, m] += legendre_back(recv2[:, m], leg[m])
+    peers(functools.partial(depart, 3), HELD, 31)
+
+    all2(0).wait_recv()
+    all2(1).wait_recv()
+    for m in range(WAVE):
+        if m % 2 == 0:
+            back = recv2[:, :, 8 * m : 8 * m + 16].astype(F32)
+        rows = slice(m % 2 * 8, m % 2 * 8 + 8)
+        spec[0, m] += legendre_back(back[0, :, rows], back[1, :, rows], leg[m])
         pltpu.make_async_copy(spec.at[0, m], done_hbm.at[m], out_sem.at[0, m]).start()
-
-    all2(0).wait_recv()
-    for m in range(WAVE):
-        finish(m)
     all_z().wait_recv()
-    total[mine] = lax.fori_loop(1, Z, lambda i, t: t + got_z[i], got_z[0])
+    total[mine] = sum_of(got_z, Z)
     each(1, 32, lambda s: copy_c(s).start())
     own.wait()
-    for b in range(TRAJ):
-        all1(b).wait_send()
-        all2(b).wait_send()
+    for q in range(2 * TRAJ):
+        all1(q).wait_send()
+        all2(q).wait_send()
     for m in range(WAVE):
         pltpu.make_async_copy(spec.at[0, m], done_hbm.at[m], out_sem.at[0, m]).wait()
         pltpu.make_async_copy(spec.at[1, m], spec_hbm.at[m], out_sem.at[1, m]).wait()
@@ -339,21 +363,25 @@
     all_z().wait_send()
     all_c().wait_recv()
     all_c().wait_send()
-    all2(1).wait_recv()
+    all2(2).wait_recv()
+    all2(3).wait_recv()
 
 
 def last_kernel(
     done_hbm, spec_hbm, back_hbm, leg_hbm, total_hbm,
     out_hbm, g_in, g_bin, g_mid, g_bmid, g_out,
-    held, spec, back, leg, total, sem, out_sem, done_sem, total_sem,
+    held, spec, back, leg, total, sem, pair_sem, out_sem, done_sem, total_sem,
 ):
     done = pltpu.make_async_copy(done_hbm, held, done_sem.at[0])
     store = pltpu.make_async_copy(held, out_hbm.at[0], done_sem.at[1])
+    pairs = [
+        pltpu.make_async_copy(back_hbm.at[:, :, rows], back.at[:, :, rows], pair_sem.at[p])
+        for p, rows in enumerate([pl.ds(0, 16), pl.ds(16, 16), pl.ds(32, 16)])
+    ]
     loads = [
-        [
-            pltpu.make_async_copy(back_hbm.at[:, m], back.at[:, m], sem.at[m, 0]),
-            pltpu.make_async_copy(leg_hbm.at[m], leg.at[m], sem.at[m, 1]),
-            pltpu.make_async_copy(spec_hbm.at[m], spec.at[m], sem.at[m, 2]),
+        ([pairs[m // 2]] if m % 2 == 0 else []) + [
+            pltpu.make_async_copy(leg_hbm.at[m], leg.at[m], sem.at[m, 0]),
+            pltpu.make_async_copy(spec_hbm.at[m], spec.at[m], sem.at[m, 1]),
         ]
         for m in range(WAVE)
     ]
@@ -368,24 +396,28 @@
     for m in range(WAVE):
         for load in loads[m]:
             load.wait()
-        spec[m] += legendre_back(back[:, m], leg[m])
+        if m % 2 == 0:
+            wide = back[:, :, 8 * m : 8 * m + 16].astype(F32)
+        rows = slice(m % 2 * 8, m % 2 * 8 + 8)
+        spec[m] += legendre_back(wide[0, :, rows], wide[1, :, rows], leg[m])
         stores.append(pltpu.make_async_copy(spec.at[m], out_hbm.at[1, m], out_sem.at[m]))
         stores[-1].start()
         if m == 0:
             done.wait()
             store.start()
     sums.wait()
-    squares = total[...] * total[...]
+    whole = total[...].astype(F32)
+    squares = whole * whole
     factor = jnp.minimum(F32(1.0), LIMIT / jnp.sqrt(jnp.sum(squares, keepdims=True) + 1e-06))
-    g_in[:, :128] = factor * total[0:128]
-    g_in[:, 128:] = factor * total[128:256]
-    g_mid[:, :128] = factor * total[256:512]
-    g_mid[:, 128:] = factor * total[512:768]
-    g_out[...] = factor * total[768:1024]
-    g_bin[:, :128] = factor * total[1024:1025]
-    g_bin[:, 128:] = factor * total[1025:1026]
-    g_bmid[:, :128] = factor * total[1026:1027]
-    g_bmid[:, 128:] = factor * total[1027:1028]
+    g_in[:, :128] = factor * whole[0:128]
+    g_in[:, 128:] = factor * whole[128:256]
+    g_mid[:, :128] = factor * whole[256:512]
+    g_mid[:, 128:] = factor * whole[512:768]
+    g_out[...] = factor * whole[768:1024]
+    g_bin[:, :128] = factor * whole[1024:1025]
+    g_bin[:, 128:] = factor * whole[1025:1026]
+    g_bmid[:, :128] = factor * whole[1026:1027]
+    g_bmid[:, 128:] = factor * whole[1027:1028]
     for store in stores:
         store.wait()
 
@@ -397,7 +429,7 @@
     vmem = pl.BlockSpec(memory_space=pltpu.VMEM)
     hbm = pl.BlockSpec(memory_space=pl.ANY)
     cols = TRAJ * LATS
-    message = (TRAJ, SP, WAVE, 2 * LATS, CHAN)
+    message = (2 * TRAJ, SP, 2 * WAVE * HALF, CHAN)
     dma = pltpu.SemaphoreType.DMA
     state_half = jax.ShapeDtypeStruct((WAVE, CHAN, COEF), F32)
     done, spec, back, total = pl.pallas_call(
@@ -406,8 +438,8 @@
         out_shape=(
             state_half,
             state_half,
-            jax.ShapeDtypeStruct(message[1:], BF16),
-            jax.ShapeDtypeStruct((ROWS, 128), F32),
+            jax.ShapeDtypeStruct((2, *message[1:]), BF16),
+            jax.ShapeDtypeStruct((ROWS, 128), BF16),
         ),
         in_specs=[hbm] * 11,
         out_specs=[hbm] * 3 + [vmem],
@@ -428,8 +460,8 @@
             pltpu.VMEM(message, BF16),
             pltpu.VMEM(message, BF16),
             pltpu.VMEM(message, BF16),
-            pltpu.VMEM(message[1:], BF16),
-            pltpu.VMEM((MC * LATS, CHAN), F32),
+            pltpu.VMEM((2, *message[1:]), BF16),
+            pltpu.VMEM((MC * HALF, CHAN), F32),
             pltpu.VMEM((cols, HIDDEN, LONS), BF16),
             pltpu.VMEM((cols, HIDDEN, LONS), BF16),
             pltpu.VMEM((cols, HIDDEN, LONS), F32),
@@ -442,15 +474,16 @@
             pltpu.VMEM((ROWS, 128), F32),
             pltpu.VMEM((HIDDEN, 128), F32),
             pltpu.VMEM((HIDDEN, 128), F32),
-            pltpu.VMEM((32, SEG, 128), F32),
-            pltpu.VMEM((Z, SEG, 128), F32),
+            pltpu.VMEM((ROWS, 128), BF16),
+            pltpu.VMEM((32, SEG, 128), BF16),
+            pltpu.VMEM((Z, SEG, 128), BF16),
             dma((12,)),
             dma((TRAJ, WAVE)),
             dma,
-            dma((TRAJ,)),
-            dma((TRAJ,)),
-            dma((TRAJ,)),
-            dma((TRAJ,)),
+            dma((2 * TRAJ,)),
+            dma((2 * TRAJ,)),
+            dma((2 * TRAJ,)),
+            dma((2 * TRAJ,)),
             dma,
             dma,
             dma,
@@ -481,10 +514,11 @@
         scratch_shapes=[
             pltpu.VMEM((WAVE, CHAN, COEF), F32),
             pltpu.VMEM((WAVE, CHAN, COEF), F32),
-            pltpu.VMEM(message[1:], BF16),
+            pltpu.VMEM((2, *message[1:]), BF16),
             pltpu.VMEM((WAVE, DEG, LATS * SP), BF16),
-            pltpu.VMEM((ROWS, 128), F32),
-            dma((WAVE, 3)),
+            pltpu.VMEM((ROWS, 128), BF16),
+            dma((WAVE, 2)),
+            dma((3,)),
             dma((WAVE,)),
             dma((2,)),
             dma,

time: 99.3 us -> 96.2 us (0.969)
  Pallas kernels: 98.6 us -> 95.3 us
    pallas_call x1, Pallas kernels: 93.2 us -> 89.9 us  [shards(): pl.pallas_call(kernel, name='exchange', out_shape=(state_half, state_half...]
where the time goes in v3:
time: 96.2 us; the launch traced here: 96.1 us
  Pallas kernels  95.3 us (99%)
    pallas_call x1, Pallas kernels, shards(): pl.pallas_call(kernel, name='exchange', out_shape=(state_half, state_half...  89.9 us
    pallas_call x1, Pallas kernels, shards(): pl.pallas_call(last_kernel, name='finish', out_shape=(jax.ShapeDtypeStruc...  5.32 us

profile of v3, /device:TPU:1, one launch (start us, length us, event | category | flops | bytes accessed | tf_op | source)
XLA Modules:
  0.0 96.1 jit_solution(13644747798588316966)
XLA Ops:
  0.6 89.9 %exchange.1 = (f32[6,128,384]{2,1,0:T(8,128)}, f32[6,128,384]{2,1,0:T(8,128)}, bf16[2,32,48,128]{3,2,1,0:T(8,128)(2,1)}, bf16[1536,128]{1,0:T(8,128)(2,1)}) custom-call(f32[2,6,128,384]{3,2,1,0:T(8,128)} %cot_hbm.1, bf16[2,8,128,512]{3,2,1,0:T(8,128)(2,1)} %grid_hbm.1, bf16[6,192,256]{2,1,0:T(8,128)(2,1)} %leg_hbm.3, f32[6,4,32,32]{3,2,1,0:T(8,128)} %inv_hbm.1, ...), custom_call_target="tpu_custom_call" | custom-call | tf_op jit(solution)/shard_map/exchange/pallas_call | solution.py:435
  90.6 5.3 %finish.1 = (f32[2,6,128,384]{3,2,1,0:T(8,128)}, f32[128,256]{1,0:T(8,128)}, f32[1,256]{1,0:T(1,128)}, f32[256,256]{1,0:T(8,128)}, f32[1,256]{1,0:T(1,128)}, /*index=5*/f32[256,128]{1,0:T(8,128)}) custom-call(f32[6,128,384]{2,1,0:T(8,128)} %get-tuple-element.16.done_hbm, f32[6,128,384]{2,1,0:T(8,128)} %get-tuple-element.17.spec_hbm, ...), custom_call_target="tpu_custom_call" | custom-call | tf_op jit(solution)/shard_map/finish/pallas_call | solution.py:501

commit v4 on v2

--- a/solution.py
+++ b/solution.py
@@ -19,7 +19,7 @@
 CHAN, HIDDEN, LONS, DEG = 128, 256, 512, 192
 COEF = 2 * DEG
 MC = 2 * WAVE * SP
-SEG = 40
+SEG = 48
 ROWS = 32 * SEG
 HELD = 16
 LIMIT = math.sqrt(2 * CHAN * HIDDEN + HIDDEN * HIDDEN + 2 * HIDDEN)
@@ -59,19 +59,25 @@
     return jnp.concatenate([sums[:CHAN], sums[CHAN:]], axis=1)
 
 
+def sum_of(ref, count):
+    first = ref[0].astype(F32)
+    whole = lax.fori_loop(1, count, lambda i, t: t + ref[i].astype(F32), first)
+    return whole.astype(BF16)
+
+
 def kernel(
     cot_hbm, grid_hbm, leg_hbm, inv_hbm, gw_hbm, w_in_hbm, b_in_hbm, w_mid_hbm, b_mid_hbm, w_out_hbm,
-    tab_hbm, done_hbm, spec_hbm, back_hbm, total,
+    tab_hbm, done_hbm, spec_hbm, back_hbm, total_hbm,
     cot, grid, leg, inv, gw, w_in, b_in, w_mid, b_mid, w_out, tab,
     spec, solve, send1, recv1, send2, recv2, wide,
     h_in, h_mid, s_in, s_mid, w_in_t, w_mid_t, col_g, col_in, col_mid,
-    acc, acc_bin, acc_bmid, got_a, got_z,
-    in_sem, out_sem, own_sem,
+    acc, acc_bin, acc_bmid, parts, got_a, got_z, summed,
+    in_sem, out_sem, own_sem, sum_sem, ready,
     s1_sem, r1_sem, s2_sem, r2_sem, sa_sem, ra_sem, sz_sem, rz_sem, sc_sem, rc_sem,
 ):
     me = lax.axis_index("space")
     bat = lax.axis_index("batch")
-    z, x = me // X, me % X
+    z, x = lax.div(me, X), lax.rem(me, X)
     gi = bat * X + x
 
     loads = [
@@ -82,27 +88,23 @@
             (b_mid_hbm, b_mid), (grid_hbm, grid), (w_out_hbm, w_out), (tab_hbm, tab),
         ])
     ]
-    for load in loads:
+    for load in loads[:4]:
         load.start()
 
     def shift(t):
-        i, g = t % 8, t // 8
-        return 4 + (1 - 2 * (i % 2)) * ((i + 1) // 2), g + i // 2
+        i, g = lax.rem(t, 8), lax.div(t, 8)
+        return 4 + (1 - 2 * lax.rem(i, 2)) * lax.div(i + 1, 2), g + lax.div(i, 2)
 
     def space_peer(t):
         dz, dx = shift(t)
-        return (z + dz) % Z * X + (x + dx) % X
-
-    def space_source(t):
-        dz, dx = shift(t)
-        return (z - dz + Z) % Z * X + (x - dx + 2 * X) % X
+        return lax.rem(z + dz, Z) * X + lax.rem(x + dx, X)
 
     def group_peer(s):
-        g = (gi + s) % 32
-        return g, (z * X + g % X, g // X)
+        g = lax.rem(gi + s, 32)
+        return g, (z * X + lax.rem(g, X), lax.div(g, X))
 
     def depth_peer(s):
-        return (z + s) % Z * X + x
+        return lax.rem(z + s, Z) * X + x
 
     def each(first, last, act, unroll=1):
         def body(s, carry):
@@ -112,18 +114,23 @@
         lax.fori_loop(first, last, body, 0, unroll=unroll)
 
     def peers(act, first=0, last=31):
-        each(first, last, lambda t: act(t + (t + 17) // 32))
+        each(first, last, lambda t: act(t + lax.div(t + 17, 32)))
 
     barrier = pltpu.get_barrier_semaphore()
 
     def greet(t):
         pl.semaphore_signal(barrier, inc=1, device_id=(space_peer(t), bat), device_id_type=MESH)
 
-    def greet_group(s):
-        pl.semaphore_signal(barrier, inc=1, device_id=group_peer(s)[1], device_id_type=MESH)
+    def greet_batch(s):
+        where = (me, lax.rem(bat + s, NB))
+        pl.semaphore_signal(barrier, inc=1, device_id=where, device_id_type=MESH)
+
+    def confirm(s):
+        where = (z * X + lax.rem(x + s, X), bat)
+        pl.semaphore_signal(ready, inc=1, device_id=where, device_id_type=MESH)
 
     peers(greet)
-    each(1, 32, greet_group)
+    each(1, NB, greet_batch)
 
     def copy1(b, s):
         peer = space_peer(s)
@@ -144,7 +151,7 @@
     def copy_a(s):
         g, where = group_peer(s)
         return pltpu.make_async_remote_copy(
-            src_ref=acc.at[pl.ds(pl.multiple_of(g * SEG, 8), SEG)], dst_ref=got_a.at[gi],
+            src_ref=parts.at[pl.ds(pl.multiple_of(g * SEG, SEG), SEG)], dst_ref=got_a.at[gi],
             send_sem=sa_sem, recv_sem=ra_sem, device_id=where, device_id_type=MESH,
         )
 
@@ -157,9 +164,9 @@
 
     def copy_c(s):
         _, where = group_peer(s)
-        mine = pl.ds(pl.multiple_of(gi * SEG, 8), SEG)
+        mine = pl.ds(pl.multiple_of(gi * SEG, SEG), SEG)
         return pltpu.make_async_remote_copy(
-            src_ref=total.at[mine], dst_ref=total.at[mine],
+            src_ref=summed, dst_ref=total_hbm.at[mine],
             send_sem=sc_sem, recv_sem=rc_sem, device_id=where, device_id_type=MESH,
         )
 
@@ -179,14 +186,14 @@
         return bulk(send2.at[b, part], target, s2_sem.at[b], r2_sem.at[b])
 
     def all_a():
-        return bulk(acc.at[pl.ds(0, 31 * SEG)], got_a.at[pl.ds(0, 31)], sa_sem, ra_sem)
+        return bulk(parts.at[pl.ds(0, 31 * SEG)], got_a.at[pl.ds(0, 31)], sa_sem, ra_sem)
 
     def all_z():
         return bulk(got_z.at[pl.ds(0, Z - 1)], got_z.at[pl.ds(0, Z - 1)], sz_sem, rz_sem)
 
     def all_c():
         part = pl.ds(0, 31 * SEG)
-        return bulk(total.at[part], total.at[part], sc_sem, rc_sem)
+        return bulk(parts.at[part], total_hbm.at[part], sc_sem, rc_sem)
 
     lane = lax.broadcasted_iota(jnp.int32, (32, CHAN), 1)
     row = lax.broadcasted_iota(jnp.int32, (32, CHAN), 0)
@@ -221,6 +228,8 @@
 
     for load in loads[:4]:
         load.wait()
+    for load in loads[4:]:
+        load.start()
     col_g[...] = column(gw)
     for b in range(TRAJ):
         if b == 1:
@@ -228,8 +237,10 @@
         for m in range(WAVE):
             spectral_in(b, m)
         if b == 0:
-            pl.semaphore_wait(barrier, 62)
-        peers(lambda t: copy1(b, t).start())
+            pl.semaphore_wait(barrier, SP - 1 + NB - 1)
+        if b == 0:
+            peers(lambda t: copy1(0, t).start())
+            each(1, X, confirm)
         recv1[b, me] = send1[b, me]
 
     for load in loads[5:]:
@@ -243,6 +254,8 @@
     acc_bmid[...] = jnp.zeros_like(acc_bmid)
     def forward(i):
         b, a = i // LATS, i % LATS
+        first = 2 * i
+        peers(lambda t: copy1(1, t).start(), first, jnp.minimum(first + 2, 31))
         pre = dot(w_in_t[...], grid[b, a], 1, 0)
         value, slope = gelu_pair(pre + jnp.concatenate([col_in[...]] * 4, axis=1))
         hidden = value.astype(BF16)
@@ -289,7 +302,7 @@
     for b in range(TRAJ):
         all1(b).wait_recv()
         each(0, SP, functools.partial(unpack, b), 4)
-        each(0, LATS, functools.partial(backward, b), 2)
+        each(0, LATS, functools.partial(backward, b), 4)
 
         def depart(t):
             pack(b, space_peer(t))
@@ -306,15 +319,17 @@
     acc[1025:1026] = bins[:, 128:]
     acc[1026:1027] = bmids[:, :128]
     acc[1027:1028] = bmids[:, 128:]
+    parts[...] = acc[...].astype(BF16)
+    pl.semaphore_wait(ready, X - 1)
     each(1, 32, lambda s: copy_a(s).start())
     peers(depart, 0, HELD)
     pack(1, me)
     own = pltpu.make_async_copy(send2.at[1, me], back_hbm.at[me], own_sem)
     own.start()
-    mine = pl.ds(pl.multiple_of(gi * SEG, 8), SEG)
-    got_a[gi] = acc[mine]
+    mine = pl.ds(pl.multiple_of(gi * SEG, SEG), SEG)
+    got_a[gi] = parts[mine]
     all_a().wait_recv()
-    got_z[z] = lax.fori_loop(1, 32, lambda i, t: t + got_a[i], got_a[0])
+    got_z[z] = sum_of(got_a, 32)
     each(1, Z, lambda s: copy_z(s).start())
     peers(depart, HELD, 31)
 
@@ -326,9 +341,12 @@
     for m in range(WAVE):
         finish(m)
     all_z().wait_recv()
-    total[mine] = lax.fori_loop(1, Z, lambda i, t: t + got_z[i], got_z[0])
+    summed[...] = sum_of(got_z, Z)
+    own_sum = pltpu.make_async_copy(summed, total_hbm.at[mine], sum_sem)
+    own_sum.start()
     each(1, 32, lambda s: copy_c(s).start())
     own.wait()
+    own_sum.wait()
     for b in range(TRAJ):
         all1(b).wait_send()
         all2(b).wait_send()
@@ -344,11 +362,12 @@
 
 def last_kernel(
     done_hbm, spec_hbm, back_hbm, leg_hbm, total_hbm,
-    out_hbm, g_in, g_bin, g_mid, g_bmid, g_out,
-    held, spec, back, leg, total, sem, out_sem, done_sem, total_sem,
+    out_hbm, in_hbm, bin_hbm, mid_hbm, bmid_hbm, wout_hbm,
+    g_in, g_bin, g_mid, g_bmid, g_out, held, spec, back, leg, total,
+    sem, out_sem, done_sem, total_sem, grad_sem,
 ):
     done = pltpu.make_async_copy(done_hbm, held, done_sem.at[0])
-    store = pltpu.make_async_copy(held, out_hbm.at[0], done_sem.at[1])
+    stores = [pltpu.make_async_copy(held, out_hbm.at[0], done_sem.at[1])]
     loads = [
         [
             pltpu.make_async_copy(back_hbm.at[:, m], back.at[:, m], sem.at[m, 0]),
@@ -358,34 +377,37 @@
         for m in range(WAVE)
     ]
     sums = pltpu.make_async_copy(total_hbm, total, total_sem)
-    for load in loads[0]:
+    sums.start()
+    for load in sum(loads, []):
         load.start()
     done.start()
-    for load in sum(loads[1:], []):
-        load.start()
-    sums.start()
-    stores = [store]
+    sums.wait()
+    whole = total[...].astype(F32)
+    squares = whole * whole
+    factor = jnp.minimum(F32(1.0), LIMIT / jnp.sqrt(jnp.sum(squares, keepdims=True) + 1e-06))
+    g_in[:, :128] = factor * whole[0:128]
+    g_in[:, 128:] = factor * whole[128:256]
+    g_mid[:, :128] = factor * whole[256:512]
+    g_mid[:, 128:] = factor * whole[512:768]
+    g_out[...] = factor * whole[768:1024]
+    g_bin[:, :128] = factor * whole[1024:1025]
+    g_bin[:, 128:] = factor * whole[1025:1026]
+    g_bmid[:, :128] = factor * whole[1026:1027]
+    g_bmid[:, 128:] = factor * whole[1027:1028]
+    for i, (source, target) in enumerate([
+        (g_in, in_hbm), (g_bin, bin_hbm), (g_mid, mid_hbm), (g_bmid, bmid_hbm), (g_out, wout_hbm),
+    ]):
+        stores.append(pltpu.make_async_copy(source, target, grad_sem.at[i]))
+        stores[-1].start()
     for m in range(WAVE):
         for load in loads[m]:
             load.wait()
         spec[m] += legendre_back(back[:, m], leg[m])
         stores.append(pltpu.make_async_copy(spec.at[m], out_hbm.at[1, m], out_sem.at[m]))
         stores[-1].start()
-        if m == 0:
+        if m == 1:
             done.wait()
-            store.start()
-    sums.wait()
-    squares = total[...] * total[...]
-    factor = jnp.minimum(F32(1.0), LIMIT / jnp.sqrt(jnp.sum(squares, keepdims=True) + 1e-06))
-    g_in[:, :128] = factor * total[0:128]
-    g_in[:, 128:] = factor * total[128:256]
-    g_mid[:, :128] = factor * total[256:512]
-    g_mid[:, 128:] = factor * total[512:768]
-    g_out[...] = factor * total[768:1024]
-    g_bin[:, :128] = factor * total[1024:1025]
-    g_bin[:, 128:] = factor * total[1025:1026]
-    g_bmid[:, :128] = factor * total[1026:1027]
-    g_bmid[:, 128:] = factor * total[1027:1028]
+            stores[0].start()
     for store in stores:
         store.wait()
 
@@ -394,7 +416,6 @@
     cotangent, grid_state, legendre, inverse, gauss_weights, w_in, bias_in, w_mid, bias_mid, w_out
 ):
     table = jnp.asarray(fourier_rows(), F32).astype(BF16)
-    vmem = pl.BlockSpec(memory_space=pltpu.VMEM)
     hbm = pl.BlockSpec(memory_space=pl.ANY)
     cols = TRAJ * LATS
     message = (TRAJ, SP, WAVE, 2 * LATS, CHAN)
@@ -407,10 +428,10 @@
             state_half,
             state_half,
             jax.ShapeDtypeStruct(message[1:], BF16),
-            jax.ShapeDtypeStruct((ROWS, 128), F32),
+            jax.ShapeDtypeStruct((ROWS, 128), BF16),
         ),
         in_specs=[hbm] * 11,
-        out_specs=[hbm] * 3 + [vmem],
+        out_specs=[hbm] * 4,
         scratch_shapes=[
             pltpu.VMEM((TRAJ, WAVE, CHAN, COEF), F32),
             pltpu.VMEM((TRAJ, LATS, CHAN, LONS), BF16),
@@ -442,11 +463,15 @@
             pltpu.VMEM((ROWS, 128), F32),
             pltpu.VMEM((HIDDEN, 128), F32),
             pltpu.VMEM((HIDDEN, 128), F32),
-            pltpu.VMEM((32, SEG, 128), F32),
-            pltpu.VMEM((Z, SEG, 128), F32),
+            pltpu.VMEM((ROWS, 128), BF16),
+            pltpu.VMEM((32, SEG, 128), BF16),
+            pltpu.VMEM((Z, SEG, 128), BF16),
+            pltpu.VMEM((SEG, 128), BF16),
             dma((12,)),
             dma((TRAJ, WAVE)),
             dma,
+            dma,
+            pltpu.SemaphoreType.REGULAR,
             dma((TRAJ,)),
             dma((TRAJ,)),
             dma((TRAJ,)),
@@ -477,17 +502,23 @@
             jax.ShapeDtypeStruct((HIDDEN, CHAN), F32),
         ),
         in_specs=[hbm] * 5,
-        out_specs=[hbm] + [vmem] * 5,
+        out_specs=[hbm] * 6,
         scratch_shapes=[
+            pltpu.VMEM((CHAN, HIDDEN), F32),
+            pltpu.VMEM((1, HIDDEN), F32),
+            pltpu.VMEM((HIDDEN, HIDDEN), F32),
+            pltpu.VMEM((1, HIDDEN), F32),
+            pltpu.VMEM((HIDDEN, CHAN), F32),
             pltpu.VMEM((WAVE, CHAN, COEF), F32),
             pltpu.VMEM((WAVE, CHAN, COEF), F32),
             pltpu.VMEM(message[1:], BF16),
             pltpu.VMEM((WAVE, DEG, LATS * SP), BF16),
-            pltpu.VMEM((ROWS, 128), F32),
+            pltpu.VMEM((ROWS, 128), BF16),
             dma((WAVE, 3)),
             dma((WAVE,)),
             dma((2,)),
             dma,
+            dma((5,)),
         ],
         compiler_params=pltpu.CompilerParams(vmem_limit_bytes=60 * 1024 * 1024),
     )(done, spec, back, legendre, total)

time: 99.3 us -> 91.2 us (0.918)
  Pallas kernels: 98.6 us -> 90.5 us
    pallas_call x1, Pallas kernels: 93.2 us -> 85.4 us  [shards(): pl.pallas_call(kernel, name='exchange', out_shape=(state_half, state_half...]
where the time goes in v4:
time: 91.2 us; the launch traced here: 91.1 us
  Pallas kernels  90.5 us (99%)
    pallas_call x1, Pallas kernels, shards(): pl.pallas_call(kernel, name='exchange', out_shape=(state_half, state_half...  85.4 us
    pallas_call x1, Pallas kernels, shards(): pl.pallas_call(last_kernel, name='finish', out_shape=(jax.ShapeDtypeStruc...  5.05 us

profile of v4, /device:TPU:1, one launch (start us, length us, event | category | flops | bytes accessed | tf_op | source)
XLA Modules:
  0.0 91.1 jit_solution(18312866760431527381)
XLA Ops:
  0.6 85.4 %exchange.1 = (f32[6,128,384]{2,1,0:T(8,128)}, f32[6,128,384]{2,1,0:T(8,128)}, bf16[32,6,16,128]{3,2,1,0:T(8,128)(2,1)}, bf16[1536,128]{1,0:T(8,128)(2,1)}) custom-call(f32[2,6,128,384]{3,2,1,0:T(8,128)} %cot_hbm.1, bf16[2,8,128,512]{3,2,1,0:T(8,128)(2,1)} %grid_hbm.1, bf16[6,192,256]{2,1,0:T(8,128)(2,1)} %leg_hbm.3, f32[6,4,32,32]{3,2,1,0:T(8,128)} %inv_hbm.1, ...), custom_call_target="tpu_custom_call" | custom-call | tf_op jit(solution)/shard_map/exchange/pallas_call | solution.py:424
  86.1 5.0 %finish.1 = (f32[2,6,128,384]{3,2,1,0:T(8,128)}, f32[128,256]{1,0:T(8,128)}, f32[1,256]{1,0:T(1,128)}, f32[256,256]{1,0:T(8,128)}, f32[1,256]{1,0:T(1,128)}, /*index=5*/f32[256,128]{1,0:T(8,128)}) custom-call(f32[6,128,384]{2,1,0:T(8,128)} %get-tuple-element.16.done_hbm, f32[6,128,384]{2,1,0:T(8,128)} %get-tuple-element.17.spec_hbm, ...), custom_call_target="tpu_custom_call" | custom-call | tf_op jit(solution)/shard_map/finish/pallas_call | solution.py:493

commit v5 on v4

--- a/solution.py
+++ b/solution.py
@@ -21,7 +21,7 @@
 MC = 2 * WAVE * SP
 SEG = 48
 ROWS = 32 * SEG
-HELD = 16
+HELD = 8
 LIMIT = math.sqrt(2 * CHAN * HIDDEN + HIDDEN * HIDDEN + 2 * HIDDEN)
 
 
@@ -337,14 +337,14 @@
         spec[0, m] += legendre_back(recv2[:, m], leg[m])
         pltpu.make_async_copy(spec.at[0, m], done_hbm.at[m], out_sem.at[0, m]).start()
 
-    all2(0).wait_recv()
-    for m in range(WAVE):
-        finish(m)
     all_z().wait_recv()
     summed[...] = sum_of(got_z, Z)
     own_sum = pltpu.make_async_copy(summed, total_hbm.at[mine], sum_sem)
     own_sum.start()
     each(1, 32, lambda s: copy_c(s).start())
+    all2(0).wait_recv()
+    for m in range(WAVE):
+        finish(m)
     own.wait()
     own_sum.wait()
     for b in range(TRAJ):

time: 91.2 us -> 89 us (0.976)
  Pallas kernels: 90.5 us -> 88.2 us
    pallas_call x1, Pallas kernels: 85.4 us -> 83.2 us  [shards(): pl.pallas_call(kernel, name='exchange', out_shape=(state_half, state_half...]
where the time goes in v5:
time: 89 us; the launch traced here: 88.8 us
  Pallas kernels  88.2 us (99%)
    pallas_call x1, Pallas kernels, shards(): pl.pallas_call(kernel, name='exchange', out_shape=(state_half, state_half...  83.2 us
    pallas_call x1, Pallas kernels, shards(): pl.pallas_call(last_kernel, name='finish', out_shape=(jax.ShapeDtypeStruc...  5.05 us

profile of v5, /device:TPU:1, one launch (start us, length us, event | category | flops | bytes accessed | tf_op | source)
XLA Modules:
  0.0 88.8 jit_solution(71371417920591491)
XLA Ops:
  0.6 83.2 %exchange.1 = (f32[6,128,384]{2,1,0:T(8,128)}, f32[6,128,384]{2,1,0:T(8,128)}, bf16[32,6,16,128]{3,2,1,0:T(8,128)(2,1)}, bf16[1536,128]{1,0:T(8,128)(2,1)}) custom-call(f32[2,6,128,384]{3,2,1,0:T(8,128)} %cot_hbm.1, bf16[2,8,128,512]{3,2,1,0:T(8,128)(2,1)} %grid_hbm.1, bf16[6,192,256]{2,1,0:T(8,128)(2,1)} %leg_hbm.3, f32[6,4,32,32]{3,2,1,0:T(8,128)} %inv_hbm.1, ...), custom_call_target="tpu_custom_call" | custom-call | tf_op jit(solution)/shard_map/exchange/pallas_call | solution.py:424
  83.8 5.0 %finish.1 = (f32[2,6,128,384]{3,2,1,0:T(8,128)}, f32[128,256]{1,0:T(8,128)}, f32[1,256]{1,0:T(1,128)}, f32[256,256]{1,0:T(8,128)}, f32[1,256]{1,0:T(1,128)}, /*index=5*/f32[256,128]{1,0:T(8,128)}) custom-call(f32[6,128,384]{2,1,0:T(8,128)} %get-tuple-element.16.done_hbm, f32[6,128,384]{2,1,0:T(8,128)} %get-tuple-element.17.spec_hbm, ...), custom_call_target="tpu_custom_call" | custom-call | tf_op jit(solution)/shard_map/finish/pallas_call | solution.py:493

commit v6 on v5

--- a/solution.py
+++ b/solution.py
@@ -21,7 +21,7 @@
 MC = 2 * WAVE * SP
 SEG = 48
 ROWS = 32 * SEG
-HELD = 8
+HELD = 10
 LIMIT = math.sqrt(2 * CHAN * HIDDEN + HIDDEN * HIDDEN + 2 * HIDDEN)
 
 
@@ -254,8 +254,8 @@
     acc_bmid[...] = jnp.zeros_like(acc_bmid)
     def forward(i):
         b, a = i // LATS, i % LATS
-        first = 2 * i
-        peers(lambda t: copy1(1, t).start(), first, jnp.minimum(first + 2, 31))
+        first = jnp.minimum(4 * i, 31)
+        peers(lambda t: copy1(1, t).start(), first, jnp.minimum(first + 4, 31))
         pre = dot(w_in_t[...], grid[b, a], 1, 0)
         value, slope = gelu_pair(pre + jnp.concatenate([col_in[...]] * 4, axis=1))
         hidden = value.astype(BF16)

time: 89 us -> 89.3 us (level)
  no operation moved by 1% of the time
where the time goes in v6:
time: 89.3 us; the launch traced here: 89.2 us
  Pallas kernels  88.5 us (99%)
    pallas_call x1, Pallas kernels, shards(): pl.pallas_call(kernel, name='exchange', out_shape=(state_half, state_half...  83.5 us
    pallas_call x1, Pallas kernels, shards(): pl.pallas_call(last_kernel, name='finish', out_shape=(jax.ShapeDtypeStruc...  5.04 us

profile of v6, /device:TPU:1, one launch (start us, length us, event | category | flops | bytes accessed | tf_op | source)
XLA Modules:
  0.0 89.2 jit_solution(16605651693460372317)
XLA Ops:
  0.6 83.5 %exchange.1 = (f32[6,128,384]{2,1,0:T(8,128)}, f32[6,128,384]{2,1,0:T(8,128)}, bf16[32,6,16,128]{3,2,1,0:T(8,128)(2,1)}, bf16[1536,128]{1,0:T(8,128)(2,1)}) custom-call(f32[2,6,128,384]{3,2,1,0:T(8,128)} %cot_hbm.1, bf16[2,8,128,512]{3,2,1,0:T(8,128)(2,1)} %grid_hbm.1, bf16[6,192,256]{2,1,0:T(8,128)(2,1)} %leg_hbm.3, f32[6,4,32,32]{3,2,1,0:T(8,128)} %inv_hbm.1, ...), custom_call_target="tpu_custom_call" | custom-call | tf_op jit(solution)/shard_map/exchange/pallas_call | solution.py:424
  84.1 5.0 %finish.1 = (f32[2,6,128,384]{3,2,1,0:T(8,128)}, f32[128,256]{1,0:T(8,128)}, f32[1,256]{1,0:T(1,128)}, f32[256,256]{1,0:T(8,128)}, f32[1,256]{1,0:T(1,128)}, /*index=5*/f32[256,128]{1,0:T(8,128)}) custom-call(f32[6,128,384]{2,1,0:T(8,128)} %get-tuple-element.16.done_hbm, f32[6,128,384]{2,1,0:T(8,128)} %get-tuple-element.17.spec_hbm, ...), custom_call_target="tpu_custom_call" | custom-call | tf_op jit(solution)/shard_map/finish/pallas_call | solution.py:493
